TPU v7x, 256 devices: a whole 4x4x8 slice. The times are simulated.
256 devices in a mesh: dp: 32 (over y, z), grp: 8 (over x, core).
Axes of the slice: x: 4, y: 4, z: 8, core: 2. Of those that a mesh axis runs over, the one named last changes fastest.
Arguments:
- query_in: bfloat16 [32768, 2048], P(('dp', 'grp')), may hold values from -6 to 6
- key_in: bfloat16 [32768, 2048], P(('dp', 'grp')), may hold values from -6 to 6
- value_in: bfloat16 [32768, 2048], P(('dp', 'grp')), may hold values from -6 to 6
- out_grad: bfloat16 [32768, 2048], P(('dp', 'grp')), may hold values from -6 to 6
- query_gain: float32 [128], replicated, may hold values from 1.5 to 2.5
- key_gain: float32 [128], replicated, may hold values from 1.5 to 2.5
- positions: int32 [3, 32768], P(None, ('dp', 'grp')), may hold values from 0 to 63
- token_place: int32 [32768], P(('dp', 'grp')), may hold values from 0 to 32767, as said below
- clip_index: int32 [32, 1024], P('dp'), may hold values from 0 to 1, never falling along the last dimension, each value on 1 to 768 neighbouring positions
Outputs:
- attention: bfloat16 [32768, 2048], P(('dp', 'grp'))
- grad_query: bfloat16 [32768, 2048], P(('dp', 'grp'))
- grad_key: bfloat16 [32768, 2048], P(('dp', 'grp'))
- grad_value: bfloat16 [32768, 2048], P(('dp', 'grp'))
Inputs may be any that keep to these rules, and one draw needn't show every extreme that they name: `token_place`: A permutation. Place s lies in group s // 1024 and is held by the device with dp index s // 1024 and grp index (s // 128) % 8; every token keeps its grp index. The tokens of one device go to exactly 16 dp indices, exactly 8 to each. `clip_index`: in each row, clips are runs of places numbered in order, each of 1 to 768 places.
All inputs are finite; a program needn't handle non-finite values.
Results may differ from a plain program's by a relative error of at most 0.015.
Values may be sent and summed in bfloat16 or wider, within the bound.
No kernel may reach another device: no remote copies, remote signals or barrier semaphores. Data moves between devices by JAX's collectives and lax.ppermute only.
A program may use at most 128 MiB of HBM per device.

v0:
```python
import functools
import math

import jax
import jax.numpy as jnp
from jax import lax
from jax.experimental import pallas as pl
from jax.experimental.pallas import tpu as pltpu
from jax.sharding import PartitionSpec as P

HEAD_DIM = 128
ROPE_T = 16
CAP = 8
META = 128
eps = 1e-06
rope_base = 256.0
factor = 1.0 / math.sqrt(HEAD_DIM)
MB = 1024 * 1024


def f32_dot(a, b, dims):
    return lax.dot_general(a, b, (dims, ((), ())), preferred_element_type=jnp.float32)


def as_column(row):
    n = row.shape[1]
    eye = lax.broadcasted_iota(jnp.int32, (n, n), 0) == lax.broadcasted_iota(jnp.int32, (n, n), 1)
    return jnp.sum(jnp.where(eye, jnp.broadcast_to(row, (n, n)), 0.0), axis=1, keepdims=True)


def slot_of_token(place_row, group_rows):
    n = place_row.shape[1]
    target = (place_row // group_rows).astype(jnp.float32)
    column = as_column(target)
    earlier = lax.broadcasted_iota(jnp.int32, (n, n), 0) < lax.broadcasted_iota(
        jnp.int32, (n, n), 1
    )
    same = (column == jnp.broadcast_to(target, (n, n))) & earlier
    rank = jnp.sum(jnp.where(same, 1.0, 0.0), axis=0, keepdims=True)
    return target * CAP + rank


def rotation(positions):
    n = positions.shape[1]
    channel = lax.broadcasted_iota(jnp.int32, (1, HEAD_DIM), 1)
    pair = channel // 2
    time_pairs = ROPE_T // 2
    space_pairs = (HEAD_DIM - ROPE_T) // 4
    first = pair < time_pairs
    second = pair < time_pairs + space_pairs
    offset = jnp.where(first, 0, jnp.where(second, time_pairs, time_pairs + space_pairs))
    span = jnp.where(first, float(ROPE_T), float((HEAD_DIM - ROPE_T) // 2))
    frequency = jnp.exp(
        (-2.0 * math.log(rope_base)) * (pair - offset).astype(jnp.float32) / span
    )
    rows = positions.astype(jnp.float32)
    shape = (n, HEAD_DIM)
    columns = [jnp.broadcast_to(as_column(rows[i : i + 1]), shape) for i in range(3)]
    chosen = jnp.where(first, columns[0], jnp.where(second, columns[1], columns[2]))
    angles = chosen * frequency
    sine = jnp.sin(angles)
    odd = (channel % 2) == 1
    return jnp.cos(angles), jnp.where(odd, sine, -sine)


def swap_pairs(values):
    odd = (lax.broadcasted_iota(jnp.int32, values.shape, 1) % 2) == 1
    down = pltpu.roll(values, 1, axis=1)
    up = pltpu.roll(values, HEAD_DIM - 1, axis=1)
    return jnp.where(odd, down, up)


def norm_factor(values):
    return lax.rsqrt(jnp.mean(values * values, axis=-1, keepdims=True) + eps)


def pack_kernel(
    group_rows,
    query_ref,
    key_ref,
    value_ref,
    grad_ref,
    query_gain_ref,
    key_gain_ref,
    positions_ref,
    place_ref,
    out_ref,
    cosine_ref,
    sine_ref,
    pick_ref,
    meta_ref,
):
    slots = pick_ref.shape[0]
    n = query_ref.shape[0]
    dp_count = slots // CAP

    @pl.when(pl.program_id(0) == 0)
    def _():
        cosine, sine = rotation(positions_ref[...])
        cosine_ref[...] = cosine
        sine_ref[...] = sine
        place = place_ref[...]
        slot = slot_of_token(place, group_rows).astype(jnp.int32)
        pick = lax.broadcasted_iota(jnp.int32, (slots, n), 0) == jnp.broadcast_to(slot, (slots, n))
        pick = jnp.where(pick, 1.0, 0.0).astype(jnp.bfloat16)
        pick_ref[...] = pick
        code = jnp.broadcast_to((place % n + 1).astype(jnp.float32), (META, n))
        meta = f32_dot(pick, code.astype(jnp.bfloat16), ((1,), (1,)))
        meta_ref[...] = meta.reshape(dp_count, CAP, META)

    pick = pick_ref[...]
    width = query_ref.shape[1]

    def prepared(ref, gain_ref):
        parts = []
        for start in range(0, width, HEAD_DIM):
            values = ref[:, start : start + HEAD_DIM].astype(jnp.float32)
            normed = values * norm_factor(values) * gain_ref[...]
            rotated = normed * cosine_ref[...] + swap_pairs(normed) * sine_ref[...]
            parts.append(rotated.astype(jnp.bfloat16))
        return jnp.concatenate(parts, axis=1)

    def put(index, rows):
        packed = f32_dot(pick, rows, ((1,), (0,))).reshape(dp_count, CAP, width)
        out_ref[:, 0, :, index * width : (index + 1) * width] = packed.astype(jnp.bfloat16)

    put(0, prepared(query_ref, query_gain_ref))
    put(1, prepared(key_ref, key_gain_ref))
    put(2, value_ref[...])
    put(3, grad_ref[...])
    out_ref[:, 0, :, 4 * width :] = meta_ref[...].astype(jnp.bfloat16)


def attend_kernel(
    arrived_ref, clip_ref, out_ref, query_ref, key_ref, value_ref, grad_ref, pick_ref, result_ref,
    key_acc, value_acc
):
    dp_count, grp_count, cap, columns = arrived_ref.shape
    rows, width = query_ref.shape
    slots = dp_count * cap
    own = rows // grp_count
    block = 256

    for g in range(grp_count):
        code = arrived_ref[:, g, :, 4 * width :].astype(jnp.float32).reshape(slots, META)
        spot = lax.broadcasted_iota(jnp.int32, (slots, own), 1) + 1
        pick = jnp.where(code == spot.astype(jnp.float32), 1.0, 0.0).astype(jnp.bfloat16)
        pick_ref[g] = pick
        for index, target in enumerate((query_ref, key_ref, value_ref, grad_ref)):
            held = arrived_ref[:, g, :, index * width : (index + 1) * width]
            held = held.astype(jnp.float32).reshape(slots, width).astype(jnp.bfloat16)
            target[g * own : (g + 1) * own, :] = f32_dot(pick, held, ((0,), (0,))).astype(
                jnp.bfloat16
            )

    is_first = (clip_ref[...] == 0).astype(jnp.float32)
    first_rows = jnp.sum(is_first, axis=1, keepdims=True)
    key_place = lax.broadcasted_iota(jnp.int32, (1, rows), 1).astype(jnp.float32)
    key_second = key_place >= first_rows

    for head in range(width // HEAD_DIM):
        lanes = slice(head * HEAD_DIM, (head + 1) * HEAD_DIM)
        key = key_ref[:, lanes]
        value = value_ref[:, lanes]
        for start in range(0, rows, block):
            part = slice(start, start + block)
            query = query_ref[part, lanes]
            grad = grad_ref[part, lanes]
            scores = f32_dot(query, key, ((1,), (1,)))
            raised = jnp.exp2(scores * (factor * math.log2(math.e)))
            place = lax.broadcasted_iota(jnp.int32, (block, 1), 0).astype(jnp.float32) + start
            second = place >= first_rows
            raised = jnp.where(second == key_second, raised, 0.0)
            weights = raised * (1.0 / jnp.sum(raised, axis=1, keepdims=True))
            weights_low = weights.astype(jnp.bfloat16)
            attended = f32_dot(weights_low, value, ((1,), (0,))).astype(jnp.bfloat16)
            result_ref[0, part, lanes] = attended
            row_dot = jnp.sum(
                grad.astype(jnp.float32) * attended.astype(jnp.float32), axis=1, keepdims=True
            )
            grad_weights = f32_dot(grad, value, ((1,), (1,)))
            grad_scores = (weights * (grad_weights - row_dot)).astype(jnp.bfloat16)
            grad_query = f32_dot(grad_scores, key, ((1,), (0,))) * factor
            result_ref[1, part, lanes] = grad_query.astype(jnp.bfloat16)
            key_part = f32_dot(grad_scores, query, ((0,), (0,)))
            value_part = f32_dot(weights_low, grad, ((0,), (0,)))
            if start == 0:
                key_acc[...] = key_part
                value_acc[...] = value_part
            else:
                key_acc[...] += key_part
                value_acc[...] += value_part
        result_ref[2, :, lanes] = (key_acc[...] * factor).astype(jnp.bfloat16)
        result_ref[3, :, lanes] = value_acc[...].astype(jnp.bfloat16)

    for g in range(grp_count):
        pick = pick_ref[g]
        for index in range(4):
            held = result_ref[index, g * own : (g + 1) * own, :]
            packed = f32_dot(pick, held, ((1,), (0,))).reshape(dp_count, cap, width)
            out_ref[:, g, :, index * width : (index + 1) * width] = packed.astype(jnp.bfloat16)


def unpack_kernel(
    group_rows,
    back_ref,
    query_ref,
    key_ref,
    query_gain_ref,
    key_gain_ref,
    positions_ref,
    place_ref,
    attention_ref,
    grad_query_ref,
    grad_key_ref,
    grad_value_ref,
    cosine_ref,
    sine_ref,
    pick_ref,
):
    dp_count, _, cap, _ = back_ref.shape
    n, width = query_ref.shape
    slots = dp_count * cap

    @pl.when(pl.program_id(0) == 0)
    def _():
        cosine, sine = rotation(positions_ref[...])
        cosine_ref[...] = cosine
        sine_ref[...] = sine
        slot = as_column(slot_of_token(place_ref[...], group_rows)).astype(jnp.int32)
        pick = jnp.broadcast_to(slot, (n, slots)) == lax.broadcasted_iota(jnp.int32, (n, slots), 1)
        pick_ref[...] = jnp.where(pick, 1.0, 0.0).astype(jnp.bfloat16)

    pick = pick_ref[...]

    def take(index):
        held = back_ref[:, 0, :, index * width : (index + 1) * width]
        held = held.astype(jnp.float32).reshape(slots, width).astype(jnp.bfloat16)
        return f32_dot(pick, held, ((1,), (0,)))

    def pulled(index, ref, gain_ref, out_ref):
        grads = take(index)
        for start in range(0, width, HEAD_DIM):
            lanes = slice(start, start + HEAD_DIM)
            values = ref[:, lanes].astype(jnp.float32)
            scale = norm_factor(values)
            grad = grads[:, lanes]
            grad = grad * cosine_ref[...] - swap_pairs(grad) * sine_ref[...]
            grad = grad * gain_ref[...]
            unit = values * scale
            along = jnp.mean(grad * unit, axis=-1, keepdims=True)
            out_ref[:, lanes] = (scale * (grad - unit * along)).astype(jnp.bfloat16)

    attention_ref[...] = take(0).astype(jnp.bfloat16)
    grad_value_ref[...] = take(3).astype(jnp.bfloat16)
    pulled(1, query_ref, query_gain_ref, grad_query_ref)
    pulled(2, key_ref, key_gain_ref, grad_key_ref)


def on_device(
    query_in, key_in, value_in, out_grad, query_gain, key_gain, positions, token_place, clip_index
):
    n, width = query_in.shape
    dp_count = lax.axis_size("dp")
    grp_count = lax.axis_size("grp")
    group_rows = n * grp_count
    slots = dp_count * CAP
    narrow = width // grp_count
    query_gain = query_gain.reshape(1, HEAD_DIM)
    key_gain = key_gain.reshape(1, HEAD_DIM)
    place = token_place.reshape(1, n)
    bf16 = jnp.bfloat16

    def whole(array):
        return pl.BlockSpec(array.shape, lambda h: (0,) * array.ndim)

    slab = pl.BlockSpec((n, narrow), lambda h: (0, h))
    sent_width = 4 * narrow + META
    small = (query_gain, key_gain, positions, place)
    turn = [pltpu.VMEM((n, HEAD_DIM), jnp.float32)] * 2

    packed = pl.pallas_call(
        functools.partial(pack_kernel, group_rows),
        name="pack",
        grid=(grp_count,),
        in_specs=[slab] * 4 + [whole(a) for a in small],
        out_specs=pl.BlockSpec((dp_count, 1, CAP, sent_width), lambda h: (0, h, 0, 0)),
        out_shape=jax.ShapeDtypeStruct((dp_count, grp_count, CAP, sent_width), bf16),
        scratch_shapes=turn
        + [pltpu.VMEM((slots, n), bf16), pltpu.VMEM((dp_count, CAP, META), jnp.float32)],
        compiler_params=pltpu.CompilerParams(vmem_limit_bytes=24 * MB),
    )(query_in, key_in, value_in, out_grad, *small)

    def exchange(array):
        flat = array.reshape((dp_count * grp_count,) + array.shape[2:])
        moved = lax.all_to_all(flat, ("dp", "grp"), split_axis=0, concat_axis=0, tiled=True)
        return moved.reshape(array.shape)

    arrived = exchange(packed)
    results = pl.pallas_call(
        attend_kernel,
        name="attend",
        out_shape=jax.ShapeDtypeStruct((dp_count, grp_count, CAP, 4 * narrow), bf16),
        scratch_shapes=[pltpu.VMEM((group_rows, narrow), bf16)] * 4
        + [
            pltpu.VMEM((grp_count, slots, n), bf16),
            pltpu.VMEM((4, group_rows, narrow), bf16),
            pltpu.VMEM((group_rows, HEAD_DIM), jnp.float32),
            pltpu.VMEM((group_rows, HEAD_DIM), jnp.float32),
        ],
        compiler_params=pltpu.CompilerParams(vmem_limit_bytes=40 * MB),
    )(arrived, clip_index)
    back = exchange(results)

    return pl.pallas_call(
        functools.partial(unpack_kernel, group_rows),
        name="unpack",
        grid=(grp_count,),
        in_specs=[pl.BlockSpec((dp_count, 1, CAP, 4 * narrow), lambda h: (0, h, 0, 0))]
        + [slab] * 2
        + [whole(a) for a in small],
        out_specs=[slab] * 4,
        out_shape=[jax.ShapeDtypeStruct((n, width), bf16)] * 4,
        scratch_shapes=turn + [pltpu.VMEM((n, slots), bf16)],
        compiler_params=pltpu.CompilerParams(vmem_limit_bytes=24 * MB),
    )(back, query_in, key_in, *small)


def solution(mesh):
    rows = P(("dp", "grp"), None)
    in_specs = (
        rows,
        rows,
        rows,
        rows,
        P(),
        P(),
        P(None, ("dp", "grp")),
        P(("dp", "grp")),
        P("dp", None),
    )

    def run(*arrays):
        return tuple(on_device(*arrays))

    return jax.shard_map(
        run, mesh=mesh, in_specs=in_specs, out_specs=(rows,) * 4, check_vma=False
    )
```

profile of v0, /device:TPU:1, one launch (start us, length us, event | category | flops | bytes accessed | tf_op | source)
XLA Modules:
  0.0 259.8 jit_solution(4564724338927026471)
XLA Ops:
  0.6 0.0 copy-start
  0.6 1.0 copy-done
  1.7 0.0 copy-start.2
  1.7 1.0 copy-done.2
  2.7 0.0 copy-start.4
  2.7 1.0 copy-done.4
  3.8 0.0 copy-start.5
  3.8 1.0 copy-done.5
  4.8 0.0 copy-start.6
  4.8 0.7 copy-done.6
  5.5 0.0 copy-start.9
  5.5 0.7 copy-done.9
  6.1 0.0 copy-start.11
  6.1 0.7 copy-done.11
  6.8 0.0 copy-start.13
  6.8 0.7 copy-done.13
  7.5 5.6 %pack.1 = bf16[32,8,8,1152]{3,2,1,0:T(8,128)(2,1)S(1)} custom-call(bf16[128,2048]{1,0:T(8,128)(2,1)S(1)} %copy-done, bf16[128,2048]{1,0:T(8,128)(2,1)S(1)} %copy-done.2, bf16[128,2048]{1,0:T(8,128)(2,1)S(1)} %copy-done.4, bf16[128,2048]{1,0:T(8,128)(2,1)S(1)} %copy-done.5, f32[1,128]{1,0:T(1,128)S(1)} %bitcast.11, f32[1,128]{1,0:T(1,128)S(1)} %bitcast.13, ...), custom_call_target="tpu_custom_call" | custom-call | tf_op jit(solution)/shard_map/pack/pallas_call | solution.py:282
  13.0 0.0 copy-start.8
  13.0 125.0 %all_to_all.10 = bf16[256,8,1152]{2,1,0:T(8,128)(2,1)S(1)} all-to-all(bf16[256,8,1152]{2,1,0:T(8,128)(2,1)S(1)} %bitcast.7), channel_id=1, replica_groups=mesh['dp'=32,'grp'=8] {'dp','grp'}, dimensions={0} | all-to-all | bytes 9437184 | tf_op jit(solution)/shard_map/all_to_all | solution.py:296
  138.0 0.0 copy-done.8
  138.0 10.7 %attend.1 = bf16[32,8,8,1024]{3,2,1,0:T(8,128)(2,1)S(1)} custom-call(bf16[32,8,8,1152]{3,2,1,0:T(8,128)(2,1)S(1)} %bitcast.8, s32[1,1024]{1,0:T(1,128)S(1)} %copy-done.8), custom_call_target="tpu_custom_call" | custom-call | tf_op jit(solution)/shard_map/attend/pallas_call | solution.py:300
  148.8 0.0 copy-start.1
  148.8 0.0 copy-start.3
  148.8 0.0 copy-start.7
  148.8 0.0 copy-start.10
  148.8 0.0 copy-start.12
  148.8 0.0 copy-start.14
  148.8 104.5 %all_to_all.11 = bf16[256,8,1024]{2,1,0:T(8,128)(2,1)S(1)} all-to-all(bf16[256,8,1024]{2,1,0:T(8,128)(2,1)S(1)} %bitcast.10), channel_id=1, replica_groups=mesh['dp'=32,'grp'=8] {'dp','grp'}, dimensions={0} | all-to-all | bytes 8388608 | tf_op jit(solution)/shard_map/all_to_all | solution.py:296
  253.3 0.0 copy-done.1
  253.3 0.0 copy-done.3
  253.3 0.0 copy-done.7
  253.3 0.0 copy-done.10
  253.4 0.0 copy-done.12
  253.4 0.0 copy-done.14
  253.4 6.4 %unpack.1 = (bf16[128,2048]{1,0:T(8,128)(2,1)}, bf16[128,2048]{1,0:T(8,128)(2,1)}, bf16[128,2048]{1,0:T(8,128)(2,1)}, bf16[128,2048]{1,0:T(8,128)(2,1)}) custom-call(bf16[32,8,8,1024]{3,2,1,0:T(8,128)(2,1)S(1)} %bitcast.9, bf16[128,2048]{1,0:T(8,128)(2,1)S(1)} %copy-done.1, bf16[128,2048]{1,0:T(8,128)(2,1)S(1)} %copy-done.3, f32[1,128]{1,0:T(1,128)S(1)} %bitcast.12, ...), custom_call_target="tpu_custom_call" | custom-call | tf_op jit(solution)/shard_map/unpack/pallas_call | solution.py:315
Async XLA Ops:
  0.6 1.0 copy-start
  1.7 1.0 copy-start.2
  2.7 1.0 copy-start.4
  3.8 1.0 copy-start.5
  4.8 0.7 copy-start.6
  5.5 0.7 copy-start.9
  6.1 0.7 copy-start.11
  6.8 0.7 copy-start.13
  13.0 125.0 %copy-start.8 = (s32[1,1024]{1,0:T(1,128)S(1)}, s32[1,1024]{1,0:T(1,128)}, u32[]{:S(2)}) copy-start(s32[1,1024]{1,0:T(1,128)} %clip_ref.1) | copy-start | bytes 12292
  148.8 104.6 %copy-start.1 = (bf16[128,2048]{1,0:T(8,128)(2,1)S(1)}, bf16[128,2048]{1,0:T(8,128)(2,1)}, u32[]{:S(2)}) copy-start(bf16[128,2048]{1,0:T(8,128)(2,1)} %query_ref.3) | copy-start | bytes 1572868
  148.8 104.6 %copy-start.3 = (bf16[128,2048]{1,0:T(8,128)(2,1)S(1)}, bf16[128,2048]{1,0:T(8,128)(2,1)}, u32[]{:S(2)}) copy-start(bf16[128,2048]{1,0:T(8,128)(2,1)} %key_ref.3) | copy-start | bytes 1572868
  148.8 104.5 %copy-start.7 = (s32[3,128]{1,0:T(4,128)S(1)}, s32[3,128]{1,0:T(4,128)}, u32[]{:S(2)}) copy-start(s32[3,128]{1,0:T(4,128)} %positions_ref.3) | copy-start | bytes 4612
  148.8 104.5 %copy-start.10 = (f32[128]{0:T(128)S(1)}, f32[128]{0:T(128)}, u32[]{:S(2)}) copy-start(f32[128]{0:T(128)} %param.13) | copy-start | bytes 1540
  148.8 104.5 %copy-start.12 = (f32[128]{0:T(128)S(1)}, f32[128]{0:T(128)}, u32[]{:S(2)}) copy-start(f32[128]{0:T(128)} %param.14) | copy-start | bytes 1540
  148.8 104.5 %copy-start.14 = (s32[128]{0:T(128)S(1)}, s32[128]{0:T(128)}, u32[]{:S(2)}) copy-start(s32[128]{0:T(128)} %param.16) | copy-start | bytes 1540
where the time goes:
time: 260 us
  blocking collectives  229 us (88%)
  Pallas kernels  22.7 us (9%)
  local copies, waits for them, and re-layouts  6.85 us (3%)
    all_to_all x2, blocking collectives, exchange(): lax.all_to_all(flat, ('dp', 'grp'), split_axis=0, concat_axis=0, tiled=True)  229 us
    pallas_call x1, Pallas kernels, on_device(): pl.pallas_call(attend_kernel, name='attend', out_shape=jax.ShapeDtypeStru...  10.7 us
    unnamed x30, local copies, waits for them, and re-layouts  6.85 us
    pallas_call x1, Pallas kernels, on_device(): pl.pallas_call(functools.partial(unpack_kernel, group_rows), name='unpack...  6.39 us
    pallas_call x1, Pallas kernels, on_device(): pl.pallas_call(functools.partial(pack_kernel, group_rows), name='pack', g...  5.55 us

commit v1 on v0

v1 whole, which is shorter than its diff:
```python
import functools
import math

import jax
import jax.numpy as jnp
from jax import lax
from jax.experimental import pallas as pl
from jax.experimental.pallas import tpu as pltpu
from jax.sharding import PartitionSpec as P

HEAD_DIM = 128
ROPE_T = 16
CAP = 8
META = 128
eps = 1e-06
rope_base = 256.0
factor = 1.0 / math.sqrt(HEAD_DIM)
MB = 1024 * 1024


def f32_dot(a, b, dims):
    return lax.dot_general(a, b, (dims, ((), ())), preferred_element_type=jnp.float32)


def as_column(row):
    n = row.shape[1]
    eye = lax.broadcasted_iota(jnp.int32, (n, n), 0) == lax.broadcasted_iota(jnp.int32, (n, n), 1)
    return jnp.sum(jnp.where(eye, jnp.broadcast_to(row, (n, n)), 0.0), axis=1, keepdims=True)


def slot_of_token(place_row, group_rows):
    n = place_row.shape[1]
    target = (place_row // group_rows).astype(jnp.float32)
    column = as_column(target)
    earlier = lax.broadcasted_iota(jnp.int32, (n, n), 0) < lax.broadcasted_iota(
        jnp.int32, (n, n), 1
    )
    same = (column == jnp.broadcast_to(target, (n, n))) & earlier
    rank = jnp.sum(jnp.where(same, 1.0, 0.0), axis=0, keepdims=True)
    return target * CAP + rank


def rotation(positions):
    n = positions.shape[1]
    channel = lax.broadcasted_iota(jnp.int32, (1, HEAD_DIM), 1)
    pair = channel // 2
    time_pairs = ROPE_T // 2
    space_pairs = (HEAD_DIM - ROPE_T) // 4
    first = pair < time_pairs
    second = pair < time_pairs + space_pairs
    offset = jnp.where(first, 0, jnp.where(second, time_pairs, time_pairs + space_pairs))
    span = jnp.where(first, float(ROPE_T), float((HEAD_DIM - ROPE_T) // 2))
    frequency = jnp.exp(
        (-2.0 * math.log(rope_base)) * (pair - offset).astype(jnp.float32) / span
    )
    rows = positions.astype(jnp.float32)
    shape = (n, HEAD_DIM)
    columns = [jnp.broadcast_to(as_column(rows[i : i + 1]), shape) for i in range(3)]
    chosen = jnp.where(first, columns[0], jnp.where(second, columns[1], columns[2]))
    angles = chosen * frequency
    sine = jnp.sin(angles)
    odd = (channel % 2) == 1
    return jnp.cos(angles), jnp.where(odd, sine, -sine)


def swap_matrix(size):
    row = lax.broadcasted_iota(jnp.int32, (size, size), 0)
    column = lax.broadcasted_iota(jnp.int32, (size, size), 1)
    return jnp.where((row ^ 1) == column, 1.0, 0.0).astype(jnp.bfloat16)


def swapped_gain(gain):
    rows = jnp.broadcast_to(gain, (8, HEAD_DIM))
    odd = (lax.broadcasted_iota(jnp.int32, rows.shape, 1) % 2) == 1
    down = pltpu.roll(rows, 1, axis=1)
    up = pltpu.roll(rows, HEAD_DIM - 1, axis=1)
    return jnp.where(odd, down, up)[0:1]


def norm_factor(values):
    return lax.rsqrt(jnp.mean(values * values, axis=-1, keepdims=True) + eps)


def pack_kernel(group_rows, *refs):
    sources, out_ref, held = refs[:8], refs[8], refs[9:17]
    sent_ref, pick_ref, meta_ref, sems, out_sems = refs[17:]
    copies = [
        pltpu.make_async_copy(source, target, sems.at[i])
        for i, (source, target) in enumerate(zip(sources, held))
    ]
    for i in (7, 6, 4, 5, 0, 1, 2, 3):
        copies[i].start()
    query_ref, key_ref, value_ref, grad_ref = held[:4]
    query_gain_ref, key_gain_ref, positions_ref, place_ref = held[4:]
    slots, n = pick_ref.shape
    grp_count = out_ref.shape[0]
    narrow = query_ref.shape[1] // grp_count

    copies[7].wait()
    place = place_ref[...]
    slot = slot_of_token(place, group_rows).astype(jnp.int32)
    pick = lax.broadcasted_iota(jnp.int32, (slots, n), 0) == jnp.broadcast_to(slot, (slots, n))
    pick_ref[...] = jnp.where(pick, 1.0, 0.0).astype(jnp.bfloat16)
    code = jnp.broadcast_to((place % n + 1).astype(jnp.float32), (META, n)).astype(jnp.bfloat16)
    meta_ref[...] = f32_dot(pick_ref[...], code, ((1,), (1,))).astype(jnp.bfloat16)
    copies[6].wait()
    cosine, sine = rotation(positions_ref[...])
    swap = swap_matrix(narrow)
    copies[4].wait()
    copies[5].wait()
    turns = [
        (gain_ref[...] * cosine, swapped_gain(gain_ref[...]) * sine)
        for gain_ref in (query_gain_ref, key_gain_ref)
    ]
    for i in (0, 1, 2, 3):
        copies[i].wait()

    sends = []
    for h in range(grp_count):
        block = slice(h * narrow, (h + 1) * narrow)
        parts = []
        for ref, (along, across) in zip((query_ref, key_ref), turns):
            rows = ref[:, block]
            other = f32_dot(rows, swap, ((1,), (0,)))
            for start in range(0, narrow, HEAD_DIM):
                lanes = slice(start, start + HEAD_DIM)
                values = rows[:, lanes].astype(jnp.float32)
                rotated = (values * along + other[:, lanes] * across) * norm_factor(values)
                parts.append(rotated.astype(jnp.bfloat16))
        rows = jnp.concatenate(parts + [value_ref[:, block], grad_ref[:, block]], axis=1)
        sent_ref[h, :, : 4 * narrow] = f32_dot(pick_ref[...], rows, ((1,), (0,))).astype(
            jnp.bfloat16
        )
        sent_ref[h, :, 4 * narrow :] = meta_ref[...]
        sends.append(pltpu.make_async_copy(sent_ref.at[h], out_ref.at[h], out_sems.at[h]))
        sends[-1].start()
    for send in sends:
        send.wait()


def attend_kernel(
    arrived_ref,
    clip_ref,
    out_ref,
    token_ref,
    pick_ref,
    query_clip_ref,
    key_clip_ref,
    weights_ref,
    scores_ref,
    by_query_ref,
    by_key_ref,
):
    grp_count, slots, _ = arrived_ref.shape
    rows, columns = token_ref.shape
    width = columns // 4
    own = rows // grp_count
    block = rows // 4
    bf16 = jnp.bfloat16

    for g in range(grp_count):
        code = arrived_ref[g, :, columns:].astype(jnp.float32)
        spot = lax.broadcasted_iota(jnp.int32, (slots, own), 1) + 1
        pick = jnp.where(code == spot.astype(jnp.float32), 1.0, 0.0).astype(bf16)
        pick_ref[g] = pick
        token_ref[g * own : (g + 1) * own, :] = f32_dot(
            pick, arrived_ref[g, :, :columns], ((0,), (0,))
        ).astype(bf16)

    first_rows = jnp.sum((clip_ref[...] == 0).astype(jnp.float32), axis=1, keepdims=True)
    place = lax.broadcasted_iota(jnp.int32, (rows, HEAD_DIM), 0).astype(jnp.float32)
    channel = lax.broadcasted_iota(jnp.int32, (rows, HEAD_DIM), 1)
    clip = jnp.where(place >= first_rows, 1, 0)
    query_clip_ref[...] = jnp.where(channel == clip, 1.0, 0.0).astype(bf16)
    key_clip_ref[...] = jnp.where(channel == 1 - clip, -4096.0, 0.0).astype(bf16)

    spans = [(0, 3 * block), (0, rows), (0, rows), (block, rows)]
    for head in range(width // HEAD_DIM):
        at = [slice(a * width + head * HEAD_DIM, a * width + (head + 1) * HEAD_DIM) for a in range(4)]
        for i, (low, high) in enumerate(spans):
            part = slice(i * block, (i + 1) * block)
            query = token_ref[part, at[0]]
            key = token_ref[low:high, at[1]]
            value = token_ref[low:high, at[2]]
            grad = token_ref[part, at[3]]
            scores = f32_dot(
                jnp.concatenate([query, query_clip_ref[part, :]], axis=1),
                jnp.concatenate([key, key_clip_ref[low:high, :]], axis=1),
                ((1,), (1,)),
            )
            raised = jnp.exp2(scores * (factor * math.log2(math.e)))
            weights = raised * (1.0 / jnp.sum(raised, axis=1, keepdims=True))
            weights_low = weights.astype(bf16)
            weights_ref[part, low:high] = weights_low
            attended = f32_dot(weights_low, value, ((1,), (0,))).astype(bf16)
            by_query_ref[part, head * HEAD_DIM : (head + 1) * HEAD_DIM] = attended
            row_dot = jnp.sum(
                grad.astype(jnp.float32) * attended.astype(jnp.float32), axis=1, keepdims=True
            )
            grad_weights = f32_dot(grad, value, ((1,), (1,)))
            grad_scores = (weights * (grad_weights - row_dot)).astype(bf16)
            scores_ref[part, low:high] = grad_scores
            grad_query = f32_dot(grad_scores, key, ((1,), (0,))) * factor
            by_query_ref[part, width + head * HEAD_DIM : width + (head + 1) * HEAD_DIM] = (
                grad_query.astype(bf16)
            )
        meets = [(0, block, 0, 3 * block), (block, 3 * block, 0, rows), (3 * block, rows, block, rows)]
        for low, high, first, last in meets:
            query = token_ref[first:last, at[0]]
            grad = token_ref[first:last, at[3]]
            channels = slice(head * HEAD_DIM, (head + 1) * HEAD_DIM)
            by_key_ref[0, channels, low:high] = (
                f32_dot(query, scores_ref[first:last, low:high], ((0,), (0,))) * factor
            ).astype(bf16)
            by_key_ref[1, channels, low:high] = f32_dot(
                grad, weights_ref[first:last, low:high], ((0,), (0,))
            ).astype(bf16)

    for g in range(grp_count):
        pick = pick_ref[g]
        part = slice(g * own, (g + 1) * own)
        out_ref[g, :, : 2 * width] = f32_dot(pick, by_query_ref[part, :], ((1,), (0,))).astype(bf16)
        for index in range(2):
            out_ref[g, :, (2 + index) * width : (3 + index) * width] = f32_dot(
                pick, by_key_ref[index, :, part], ((1,), (1,))
            ).astype(bf16)


def unpack_kernel(
    group_rows,
    back_ref,
    query_ref,
    key_ref,
    query_gain_ref,
    key_gain_ref,
    positions_ref,
    place_ref,
    *refs,
):
    outs, held, sems = refs[:4], refs[4:8], refs[8]
    grp_count, slots, _ = back_ref.shape
    n, width = query_ref.shape
    narrow = width // grp_count
    copies = [
        pltpu.make_async_copy(source, target, sems.at[i])
        for i, (source, target) in enumerate(zip(held, outs))
    ]
    slot = as_column(slot_of_token(place_ref[...], group_rows)).astype(jnp.int32)
    pick = jnp.broadcast_to(slot, (n, slots)) == lax.broadcasted_iota(jnp.int32, (n, slots), 1)
    pick = jnp.where(pick, 1.0, 0.0).astype(jnp.bfloat16)

    def take(h, index):
        rows = back_ref[h, :, index * narrow : (index + 1) * narrow]
        return f32_dot(pick, rows, ((1,), (0,)))

    for index, out in ((0, 0), (3, 3)):
        for h in range(grp_count):
            held[out][:, h * narrow : (h + 1) * narrow] = take(h, index).astype(jnp.bfloat16)
        copies[out].start()

    cosine, sine = rotation(positions_ref[...])
    swap = swap_matrix(narrow)
    for index, ref, gain_ref in ((1, query_ref, query_gain_ref), (2, key_ref, key_gain_ref)):
        along = cosine * gain_ref[...]
        across = sine * gain_ref[...]
        for h in range(grp_count):
            grads = take(h, index)
            other = f32_dot(grads.astype(jnp.bfloat16), swap, ((1,), (0,)))
            for start in range(0, narrow, HEAD_DIM):
                lanes = slice(h * narrow + start, h * narrow + start + HEAD_DIM)
                inner = slice(start, start + HEAD_DIM)
                values = ref[:, lanes].astype(jnp.float32)
                scale = norm_factor(values)
                grad = grads[:, inner] * along - other[:, inner] * across
                unit = values * scale
                share = jnp.mean(grad * unit, axis=-1, keepdims=True)
                held[index][:, lanes] = (scale * (grad - unit * share)).astype(jnp.bfloat16)
        copies[index].start()
    for copy in copies:
        copy.wait()


def on_device(
    query_in, key_in, value_in, out_grad, query_gain, key_gain, positions, token_place, clip_index
):
    n, width = query_in.shape
    dp_count = lax.axis_size("dp")
    grp_count = lax.axis_size("grp")
    group_rows = n * grp_count
    slots = dp_count * CAP
    narrow = width // grp_count
    query_gain = query_gain.reshape(1, HEAD_DIM)
    key_gain = key_gain.reshape(1, HEAD_DIM)
    place = token_place.reshape(1, n)
    bf16 = jnp.bfloat16
    vmem = pltpu.VMEM
    arguments = (query_in, key_in, value_in, out_grad, query_gain, key_gain, positions, place)
    in_hbm = pl.BlockSpec(memory_space=pltpu.HBM)
    sent_shape = (grp_count, slots, 4 * narrow + META)

    packed = pl.pallas_call(
        functools.partial(pack_kernel, group_rows),
        name="pack",
        in_specs=[in_hbm] * 8,
        out_specs=in_hbm,
        out_shape=jax.ShapeDtypeStruct(sent_shape, bf16),
        scratch_shapes=[vmem(a.shape, a.dtype) for a in arguments]
        + [
            vmem(sent_shape, bf16),
            vmem((slots, n), bf16),
            vmem((slots, META), bf16),
            pltpu.SemaphoreType.DMA((8,)),
            pltpu.SemaphoreType.DMA((grp_count,)),
        ],
        compiler_params=pltpu.CompilerParams(vmem_limit_bytes=60 * MB),
    )(*arguments)

    def exchange(array):
        flat = array.reshape(dp_count * grp_count, CAP, array.shape[2])
        moved = lax.all_to_all(flat, ("grp", "dp"), split_axis=0, concat_axis=0, tiled=True)
        return moved.reshape(array.shape)

    arrived = exchange(packed)
    results = pl.pallas_call(
        attend_kernel,
        name="attend",
        out_shape=jax.ShapeDtypeStruct((grp_count, slots, 4 * narrow), bf16),
        scratch_shapes=[
            vmem((group_rows, 4 * narrow), bf16),
            vmem((grp_count, slots, n), bf16),
            vmem((group_rows, HEAD_DIM), bf16),
            vmem((group_rows, HEAD_DIM), bf16),
            vmem((group_rows, group_rows), bf16),
            vmem((group_rows, group_rows), bf16),
            vmem((group_rows, 2 * narrow), bf16),
            vmem((2, narrow, group_rows), bf16),
        ],
        compiler_params=pltpu.CompilerParams(vmem_limit_bytes=40 * MB),
    )(arrived, clip_index)
    back = exchange(results)

    small = (query_gain, key_gain, positions, place)
    return pl.pallas_call(
        functools.partial(unpack_kernel, group_rows),
        name="unpack",
        out_specs=[in_hbm] * 4,
        out_shape=[jax.ShapeDtypeStruct((n, width), bf16)] * 4,
        scratch_shapes=[vmem((n, width), bf16)] * 4 + [pltpu.SemaphoreType.DMA((4,))],
        compiler_params=pltpu.CompilerParams(vmem_limit_bytes=24 * MB),
    )(back, query_in, key_in, *small)


def solution(mesh):
    rows = P(("dp", "grp"), None)
    in_specs = (
        rows,
        rows,
        rows,
        rows,
        P(),
        P(),
        P(None, ("dp", "grp")),
        P(("dp", "grp")),
        P("dp", None),
    )

    def run(*arrays):
        return tuple(on_device(*arrays))

    return jax.shard_map(
        run, mesh=mesh, in_specs=in_specs, out_specs=(rows,) * 4, check_vma=False
    )
```

time: 260 us -> 247 us (0.950)
  local copies, waits for them, and re-layouts: 6.85 us -> 0.04 us
  Pallas kernels: 22.7 us -> 17.2 us
    unnamed x30 -> x14, local copies, waits for them, and re-layouts: 6.85 us -> 0.04 us
    pallas_call x1, Pallas kernels: 6.39 us -> 3.15 us  [on_device(): pl.pallas_call(functools.partial(unpack_kernel, group_rows), name='unpack...]
where the time goes in v1:
time: 247 us
  blocking collectives  229 us (93%)
  Pallas kernels  17.2 us (7%)
    all_to_all x2, blocking collectives, exchange(): lax.all_to_all(flat, ('grp', 'dp'), split_axis=0, concat_axis=0, tiled=True)  229 us
    pallas_call x1, Pallas kernels, on_device(): pl.pallas_call(attend_kernel, name='attend', out_shape=jax.ShapeDtypeStru...  8.87 us
    pallas_call x1, Pallas kernels, on_device(): pl.pallas_call(functools.partial(pack_kernel, group_rows), name='pack', i...  5.14 us

profile of v1, /device:TPU:1, one launch (start us, length us, event | category | flops | bytes accessed | tf_op | source)
XLA Modules:
  0.0 247.1 jit_solution(9567071569435509734)
XLA Ops:
  0.6 5.1 %pack.1 = bf16[8,256,1152]{2,1,0:T(8,128)(2,1)} custom-call(bf16[128,2048]{1,0:T(8,128)(2,1)} %query_ref.1, bf16[128,2048]{1,0:T(8,128)(2,1)} %key_ref.1, bf16[128,2048]{1,0:T(8,128)(2,1)} %refs_2_.1, bf16[128,2048]{1,0:T(8,128)(2,1)} %refs_3_.1, f32[1,128]{1,0:T(1,128)} %bitcast.10, f32[1,128]{1,0:T(1,128)} %bitcast.12, s32[3,128]{1,0:T(4,128)} %positions_ref.1, ...), custom_call_target="tpu_custom_call" | custom-call | tf_op jit(solution)/shard_map/pack/pallas_call | solution.py:301
  5.8 0.0 copy-start.3
  5.8 124.4 %all_to_all.10 = bf16[256,8,1152]{2,1,0:T(8,128)(2,1)S(1)} all-to-all(bf16[256,8,1152]{2,1,0:T(8,128)(2,1)} %bitcast.16), channel_id=1, replica_groups=mesh['dp'=32,'grp'=8] {'grp','dp'}, dimensions={0} | all-to-all | bytes 9437184 | tf_op jit(solution)/shard_map/all_to_all | solution.py:320
  130.2 0.0 copy-done.3
  130.2 8.9 %attend.1 = bf16[8,256,1024]{2,1,0:T(8,128)(2,1)S(1)} custom-call(bf16[8,256,1152]{2,1,0:T(8,128)(2,1)S(1)} %bitcast.7, s32[1,1024]{1,0:T(1,128)S(1)} %copy-done.3), custom_call_target="tpu_custom_call" | custom-call | tf_op jit(solution)/shard_map/attend/pallas_call | solution.py:324
  139.1 0.0 copy-start
  139.1 0.0 copy-start.1
  139.1 0.0 copy-start.2
  139.1 0.0 copy-start.4
  139.1 0.0 copy-start.5
  139.1 0.0 copy-start.6
  139.1 104.6 %all_to_all.11 = bf16[256,8,1024]{2,1,0:T(8,128)(2,1)S(1)} all-to-all(bf16[256,8,1024]{2,1,0:T(8,128)(2,1)S(1)} %bitcast.9), channel_id=1, replica_groups=mesh['dp'=32,'grp'=8] {'grp','dp'}, dimensions={0} | all-to-all | bytes 8388608 | tf_op jit(solution)/shard_map/all_to_all | solution.py:320
  243.7 0.0 copy-done
  243.7 0.0 copy-done.1
  243.7 0.0 copy-done.2
  243.7 0.0 copy-done.4
  243.7 0.0 copy-done.5
  243.7 0.0 copy-done.6
  243.8 3.2 %unpack.1 = (bf16[128,2048]{1,0:T(8,128)(2,1)}, bf16[128,2048]{1,0:T(8,128)(2,1)}, bf16[128,2048]{1,0:T(8,128)(2,1)}, bf16[128,2048]{1,0:T(8,128)(2,1)}) custom-call(bf16[8,256,1024]{2,1,0:T(8,128)(2,1)S(1)} %bitcast.8, bf16[128,2048]{1,0:T(8,128)(2,1)S(1)} %copy-done, bf16[128,2048]{1,0:T(8,128)(2,1)S(1)} %copy-done.1, f32[1,128]{1,0:T(1,128)S(1)} %bitcast.11, ...), custom_call_target="tpu_custom_call" | custom-call | tf_op jit(solution)/shard_map/unpack/pallas_call | solution.py:343
Async XLA Ops:
  5.8 124.4 %copy-start.3 = (s32[1,1024]{1,0:T(1,128)S(1)}, s32[1,1024]{1,0:T(1,128)}, u32[]{:S(2)}) copy-start(s32[1,1024]{1,0:T(1,128)} %clip_ref.1) | copy-start | bytes 12292
  139.1 104.6 %copy-start = (bf16[128,2048]{1,0:T(8,128)(2,1)S(1)}, bf16[128,2048]{1,0:T(8,128)(2,1)}, u32[]{:S(2)}) copy-start(bf16[128,2048]{1,0:T(8,128)(2,1)} %query_ref.1) | copy-start | bytes 1572868
  139.1 104.6 %copy-start.1 = (bf16[128,2048]{1,0:T(8,128)(2,1)S(1)}, bf16[128,2048]{1,0:T(8,128)(2,1)}, u32[]{:S(2)}) copy-start(bf16[128,2048]{1,0:T(8,128)(2,1)} %key_ref.1) | copy-start | bytes 1572868
  139.1 104.6 %copy-start.2 = (s32[3,128]{1,0:T(4,128)S(1)}, s32[3,128]{1,0:T(4,128)}, u32[]{:S(2)}) copy-start(s32[3,128]{1,0:T(4,128)} %positions_ref.1) | copy-start | bytes 4612
  139.1 104.6 %copy-start.4 = (f32[128]{0:T(128)S(1)}, f32[128]{0:T(128)}, u32[]{:S(2)}) copy-start(f32[128]{0:T(128)} %param.13) | copy-start | bytes 1540
  139.1 104.6 %copy-start.5 = (f32[128]{0:T(128)S(1)}, f32[128]{0:T(128)}, u32[]{:S(2)}) copy-start(f32[128]{0:T(128)} %param.14) | copy-start | bytes 1540
  139.1 104.6 %copy-start.6 = (s32[128]{0:T(128)S(1)}, s32[128]{0:T(128)}, u32[]{:S(2)}) copy-start(s32[128]{0:T(128)} %param.16) | copy-start | bytes 1540

commit v2 on v1

--- a/solution.py
+++ b/solution.py
@@ -11,7 +11,8 @@
 HEAD_DIM = 128
 ROPE_T = 16
 CAP = 8
-META = 128
+Y_COUNT = 4
+Z_COUNT = 8
 eps = 1e-06
 rope_base = 256.0
 factor = 1.0 / math.sqrt(HEAD_DIM)
@@ -82,8 +83,8 @@
 
 
 def pack_kernel(group_rows, *refs):
-    sources, out_ref, held = refs[:8], refs[8], refs[9:17]
-    sent_ref, pick_ref, meta_ref, sems, out_sems = refs[17:]
+    sources, out_ref, code_ref, held = refs[:8], refs[8], refs[9], refs[10:18]
+    sent_ref, pick_ref, sems, out_sems = refs[18:]
     copies = [
         pltpu.make_async_copy(source, target, sems.at[i])
         for i, (source, target) in enumerate(zip(sources, held))
@@ -101,8 +102,11 @@
     slot = slot_of_token(place, group_rows).astype(jnp.int32)
     pick = lax.broadcasted_iota(jnp.int32, (slots, n), 0) == jnp.broadcast_to(slot, (slots, n))
     pick_ref[...] = jnp.where(pick, 1.0, 0.0).astype(jnp.bfloat16)
-    code = jnp.broadcast_to((place % n + 1).astype(jnp.float32), (META, n)).astype(jnp.bfloat16)
-    meta_ref[...] = f32_dot(pick_ref[...], code, ((1,), (1,))).astype(jnp.bfloat16)
+    rank = lax.broadcasted_iota(jnp.int32, (CAP, n), 0) == (slot & (CAP - 1))
+    code = jnp.where(rank, ((place & (n - 1)) + 1).astype(jnp.float32), 0.0).astype(jnp.bfloat16)
+    target = lax.broadcasted_iota(jnp.int32, (n, n), 0) == (slot // CAP)
+    target = jnp.where(target, 1.0, 0.0).astype(jnp.bfloat16)
+    code_ref[...] = f32_dot(code, target, ((1,), (1,))).astype(jnp.bfloat16)
     copies[6].wait()
     cosine, sine = rotation(positions_ref[...])
     swap = swap_matrix(narrow)
@@ -128,10 +132,7 @@
                 rotated = (values * along + other[:, lanes] * across) * norm_factor(values)
                 parts.append(rotated.astype(jnp.bfloat16))
         rows = jnp.concatenate(parts + [value_ref[:, block], grad_ref[:, block]], axis=1)
-        sent_ref[h, :, : 4 * narrow] = f32_dot(pick_ref[...], rows, ((1,), (0,))).astype(
-            jnp.bfloat16
-        )
-        sent_ref[h, :, 4 * narrow :] = meta_ref[...]
+        sent_ref[h] = f32_dot(pick_ref[...], rows, ((1,), (0,))).astype(jnp.bfloat16)
         sends.append(pltpu.make_async_copy(sent_ref.at[h], out_ref.at[h], out_sems.at[h]))
         sends[-1].start()
     for send in sends:
@@ -140,8 +141,13 @@
 
 def attend_kernel(
     arrived_ref,
+    near_ref,
+    mine_ref,
+    theirs_ref,
+    spot_ref,
     clip_ref,
     out_ref,
+    code_ref,
     token_ref,
     pick_ref,
     query_clip_ref,
@@ -158,14 +164,38 @@
     block = rows // 4
     bf16 = jnp.bfloat16
 
+    here, core = spot_ref[0], spot_ref[1]
+    half = Z_COUNT // 2
+    here_y, here_z = here // Z_COUNT, here & (Z_COUNT - 1)
+
+    def put_codes(ref, entry, back_z, back_y):
+        source_y = (here_y - back_y) & (Y_COUNT - 1)
+        source_z = (here_z - back_z) & (Z_COUNT - 1)
+        start = pl.multiple_of((source_y * Z_COUNT + source_z) * CAP, CAP)
+        code_ref[pl.ds(start, CAP), :] = ref[entry].astype(jnp.float32)
+
+    for back_y in range(Y_COUNT):
+        put_codes(near_ref, back_y, 0, back_y)
+        for step in range(1, half + 1):
+            entry = (step - 1) * Y_COUNT + back_y
+            put_codes(mine_ref, entry, step + (half - 1) * core, back_y)
+            put_codes(theirs_ref, entry, step + (half - 1) * (1 - core), back_y)
+
+    dp_count = slots // CAP
+    codes = code_ref[...].astype(bf16)
+    lane = lax.broadcasted_iota(jnp.int32, (rows, slots), 1)
+    grp = lax.broadcasted_iota(jnp.int32, (rows, slots), 0) // own
+    chosen = jnp.where(lane == grp * dp_count + here, 1.0, 0.0).astype(bf16)
+    by_slot = f32_dot(codes, chosen, ((1,), (1,)))
+    by_place = f32_dot(chosen, codes, ((1,), (1,)))
+    across = (lax.broadcasted_iota(jnp.int32, (slots, own), 1) + 1).astype(jnp.float32)
+    down = (lax.broadcasted_iota(jnp.int32, (own, slots), 0) + 1).astype(jnp.float32)
+
     for g in range(grp_count):
-        code = arrived_ref[g, :, columns:].astype(jnp.float32)
-        spot = lax.broadcasted_iota(jnp.int32, (slots, own), 1) + 1
-        pick = jnp.where(code == spot.astype(jnp.float32), 1.0, 0.0).astype(bf16)
-        pick_ref[g] = pick
-        token_ref[g * own : (g + 1) * own, :] = f32_dot(
-            pick, arrived_ref[g, :, :columns], ((0,), (0,))
-        ).astype(bf16)
+        part = slice(g * own, (g + 1) * own)
+        pick_ref[g] = jnp.where(by_slot[:, part] == across, 1.0, 0.0).astype(bf16)
+        pick = jnp.where(by_place[part] == down, 1.0, 0.0).astype(bf16)
+        token_ref[part, :] = f32_dot(pick, arrived_ref[g], ((1,), (0,))).astype(bf16)
 
     first_rows = jnp.sum((clip_ref[...] == 0).astype(jnp.float32), axis=1, keepdims=True)
     place = lax.broadcasted_iota(jnp.int32, (rows, HEAD_DIM), 0).astype(jnp.float32)
@@ -280,6 +310,34 @@
         copy.wait()
 
 
+def gather_codes(codes):
+    grp_count = lax.axis_size("grp")
+    here = lax.all_gather(codes, "grp", axis=0)
+    here = jnp.transpose(here, (1, 0, 2)).reshape(1, codes.shape[0], -1)
+    spots = [(y, z) for y in range(Y_COUNT) for z in range(Z_COUNT)]
+
+    def y_step(step):
+        pairs = [(y * Z_COUNT + z, (y + step) % Y_COUNT * Z_COUNT + z) for y, z in spots]
+        return lax.ppermute(here, "dp", pairs)
+
+    near = jnp.concatenate([here] + [y_step(step) for step in range(1, Y_COUNT)], axis=0)
+    half = Z_COUNT // 2
+
+    def z_step(step):
+        pairs = []
+        for y, z in spots:
+            for grp in range(grp_count):
+                target = (z + step + (half - 1) * (grp % 2)) % Z_COUNT
+                pairs.append(
+                    ((y * Z_COUNT + z) * grp_count + grp, (y * Z_COUNT + target) * grp_count + grp)
+                )
+        return lax.ppermute(near, ("dp", "grp"), pairs)
+
+    mine = jnp.concatenate([z_step(step) for step in range(1, half + 1)], axis=0)
+    theirs = lax.ppermute(mine, "grp", [(grp, grp ^ 1) for grp in range(grp_count)])
+    return near, mine, theirs
+
+
 def on_device(
     query_in, key_in, value_in, out_grad, query_gain, key_gain, positions, token_place, clip_index
 ):
@@ -296,19 +354,21 @@
     vmem = pltpu.VMEM
     arguments = (query_in, key_in, value_in, out_grad, query_gain, key_gain, positions, place)
     in_hbm = pl.BlockSpec(memory_space=pltpu.HBM)
-    sent_shape = (grp_count, slots, 4 * narrow + META)
-
-    packed = pl.pallas_call(
+    sent_shape = (grp_count, slots, 4 * narrow)
+
+    packed, codes = pl.pallas_call(
         functools.partial(pack_kernel, group_rows),
         name="pack",
         in_specs=[in_hbm] * 8,
-        out_specs=in_hbm,
-        out_shape=jax.ShapeDtypeStruct(sent_shape, bf16),
+        out_specs=[in_hbm, pl.BlockSpec(memory_space=pltpu.VMEM)],
+        out_shape=[
+            jax.ShapeDtypeStruct(sent_shape, bf16),
+            jax.ShapeDtypeStruct((CAP, n), bf16),
+        ],
         scratch_shapes=[vmem(a.shape, a.dtype) for a in arguments]
         + [
             vmem(sent_shape, bf16),
             vmem((slots, n), bf16),
-            vmem((slots, META), bf16),
             pltpu.SemaphoreType.DMA((8,)),
             pltpu.SemaphoreType.DMA((grp_count,)),
         ],
@@ -321,11 +381,16 @@
         return moved.reshape(array.shape)
 
     arrived = exchange(packed)
+    near, mine, theirs = gather_codes(codes[:, :dp_count])
+    spot = jnp.stack([lax.axis_index("dp"), lax.axis_index("grp") % 2]).astype(jnp.int32)
     results = pl.pallas_call(
         attend_kernel,
         name="attend",
+        in_specs=[pl.BlockSpec(memory_space=pltpu.VMEM)] * 4
+        + [pl.BlockSpec(memory_space=pltpu.SMEM), pl.BlockSpec(memory_space=pltpu.VMEM)],
         out_shape=jax.ShapeDtypeStruct((grp_count, slots, 4 * narrow), bf16),
         scratch_shapes=[
+            vmem((slots, slots), jnp.float32),
             vmem((group_rows, 4 * narrow), bf16),
             vmem((grp_count, slots, n), bf16),
             vmem((group_rows, HEAD_DIM), bf16),
@@ -336,7 +401,7 @@
             vmem((2, narrow, group_rows), bf16),
         ],
         compiler_params=pltpu.CompilerParams(vmem_limit_bytes=40 * MB),
-    )(arrived, clip_index)
+    )(arrived, near, mine, theirs, spot, clip_index)
     back = exchange(results)
 
     small = (query_gain, key_gain, positions, place)

time: 247 us -> 242 us (0.980)
  blocking collectives: 229 us -> 121 us
  waiting for transfers between devices: 0 us -> 64.3 us
  starting transfers between devices: 0 us -> 34 us
  Pallas kernels: 17.2 us -> 20.7 us
    all_to_all x2 -> x1, blocking collectives: 229 us -> 106 us  [exchange(): lax.all_to_all(flat, ('grp', 'dp'), split_axis=0, concat_axis=0, tiled=True)]
    ppermute x0 -> x8, waiting for transfers between devices: none -> 64.3 us  [the longest x4 60 us: z_step(): return lax.ppermute(near, ('dp', 'grp'), pairs)]
    ppermute x0 -> x8, starting transfers between devices: none -> 17.4 us  [the longest x4 12.7 us: z_step(): return lax.ppermute(near, ('dp', 'grp'), pairs)]
    all_to_all x0 -> x1, starting transfers between devices: none -> 16.7 us  [exchange(): lax.all_to_all(flat, ('grp', 'dp'), split_axis=0, concat_axis=0, tiled=True)]
    all_gather x0 -> x1, blocking collectives: none -> 15.4 us  [gather_codes(): here = lax.all_gather(codes, 'grp', axis=0)]
    pallas_call x1, Pallas kernels: 8.87 us -> 11.6 us  [on_device(): pl.pallas_call(attend_kernel, name='attend', in_specs=[pl.BlockSpec(memor...]
  transfers between devices with their start and end apart: 0 -> 9, of which waited for: 0 -> 3; matrix products, arithmetic and copies ran while one was open for 0% -> 0% of each run, Pallas kernels for 0% -> 0%
where the time goes in v2:
time: 242 us
  blocking collectives  121 us (50%)
  waiting for transfers between devices  64.3 us (27%)
  starting transfers between devices  34 us (14%)
  Pallas kernels  20.7 us (9%)
    all_to_all x1, blocking collectives, exchange(): lax.all_to_all(flat, ('grp', 'dp'), split_axis=0, concat_axis=0, tiled=True)  106 us
    ppermute x4, waiting for transfers between devices, z_step(): return lax.ppermute(near, ('dp', 'grp'), pairs)  60 us
    all_to_all x1, starting transfers between devices, exchange(): lax.all_to_all(flat, ('grp', 'dp'), split_axis=0, concat_axis=0, tiled=True)  16.7 us
    all_gather x1, blocking collectives, gather_codes(): here = lax.all_gather(codes, 'grp', axis=0)  15.4 us
    ppermute x4, starting transfers between devices, z_step(): return lax.ppermute(near, ('dp', 'grp'), pairs)  12.7 us
    pallas_call x1, Pallas kernels, on_device(): pl.pallas_call(attend_kernel, name='attend', in_specs=[pl.BlockSpec(memor...  11.6 us
    pallas_call x1, Pallas kernels, on_device(): pl.pallas_call(functools.partial(pack_kernel, group_rows), name='pack', i...  5.74 us
  transfers between devices with their start and end apart: 9, of which 3 were waited for; matrix products, arithmetic and copies ran while one was open for 0% of the time, Pallas kernels for 0%

profile of v2, /device:TPU:1, one launch (start us, length us, event | category | flops | bytes accessed | tf_op | source)
XLA Modules:
  0.0 241.7 jit_solution(1124236169209511342)
XLA Ops:
  0.6 5.7 %pack.1 = (bf16[8,256,1024]{2,1,0:T(8,128)(2,1)}, bf16[8,128]{1,0:T(8,128)(2,1)}) custom-call(bf16[128,2048]{1,0:T(8,128)(2,1)} %query_ref.1, bf16[128,2048]{1,0:T(8,128)(2,1)} %key_ref.1, bf16[128,2048]{1,0:T(8,128)(2,1)} %refs_2_.1, bf16[128,2048]{1,0:T(8,128)(2,1)} %refs_3_.1, f32[1,128]{1,0:T(1,128)} %bitcast.16, f32[1,128]{1,0:T(1,128)} %bitcast.18, ...), custom_call_target="tpu_custom_call" | custom-call | tf_op jit(solution)/shard_map/pack/pallas_call | solution.py:359
  6.4 0.0 copy-start.7
  6.4 0.0 copy-start.3
  6.4 16.7 %all-to-all-start = ((bf16[256,8,1024]{2,1,0:T(8,128)(2,1)}), bf16[256,8,1024]{2,1,0:T(8,128)(2,1)}, u32[]{:S(2)}, u32[]{:S(2)}) async-start(bf16[256,8,1024]{2,1,0:T(8,128)(2,1)} %bitcast.22), calls=%async_computation | async-start | bytes 8388608 | tf_op jit(solution)/shard_map/all_to_all | solution.py:380
  23.1 0.0 copy-done.7
  23.1 15.4 %all-gather = bf16[64,32]{1,0:T(8,128)(2,1)S(1)} all-gather(bf16[8,32]{1,0:T(8,128)(2,1)S(1)} %bitcast.25), channel_id=2, replica_groups=mesh['dp'=32,'grp'=8] {'grp'}, dimensions={0}, use_global_device_ids=true | all-gather | bytes 4608 | tf_op jit(solution)/shard_map/all_gather | solution.py:315
  38.5 0.1 reshape.37
  38.6 2.1 collective-permute-start.2
  40.7 0.4 collective-permute-start.1
  41.1 0.6 collective-permute-start
  41.7 3.5 %collective-permute-done = bf16[1,8,256]{2,1,0:T(8,128)(2,1)S(1)} collective-permute-done((bf16[1,8,256]{2,1,0:T(8,128)(2,1)S(1)}, bf16[1,8,256]{2,1,0:T(8,128)(2,1)S(1)}, u32[]{:S(2)}, u32[]{:S(2)}) %collective-permute-start) | collective-permute-done | bytes 4128 | tf_op jit(solution)/shard_map/ppermute | solution.py:321
  45.1 0.0 collective-permute-done.1
  45.1 0.0 collective-permute-done.2
  45.2 8.5 %collective-permute-start.3 = (bf16[4,8,256]{2,1,0:T(8,128)(2,1)S(1)}, bf16[4,8,256]{2,1,0:T(8,128)(2,1)S(1)}, u32[]{:S(2)}, u32[]{:S(2)}) collective-permute-start(bf16[4,8,256]{2,1,0:T(8,128)(2,1)S(1)} %constant_dynamic-update-slice_fusion.near_ref), channel_id=1, source_target_pairs={{0,8},{1,33},{2,10},{3,35},{4,12},{5,37},{6,14},{7,39},{8,16},{9,4... | collective-permute-start | bytes 49160 | tf_op jit(solution)/shard_map/ppermute | solution.py:334
  53.7 0.0 collective-permute-start.6
  53.7 0.0 collective-permute-start.5
  53.7 4.1 %collective-permute-start.4 = (bf16[4,8,256]{2,1,0:T(8,128)(2,1)S(1)}, bf16[4,8,256]{2,1,0:T(8,128)(2,1)S(1)}, u32[]{:S(2)}, u32[]{:S(2)}) collective-permute-start(bf16[4,8,256]{2,1,0:T(8,128)(2,1)S(1)} %constant_dynamic-update-slice_fusion.near_ref), channel_id=1, source_target_pairs={{0,16},{1,41},{2,18},{3,43},{4,20},{5,45},{6,22},{7,47},{8,24},{9,... | collective-permute-start | bytes 49160 | tf_op jit(solution)/shard_map/ppermute | solution.py:334
  57.8 60.0 %collective-permute-done.3 = bf16[4,8,256]{2,1,0:T(8,128)(2,1)S(1)} collective-permute-done((bf16[4,8,256]{2,1,0:T(8,128)(2,1)S(1)}, bf16[4,8,256]{2,1,0:T(8,128)(2,1)S(1)}, u32[]{:S(2)}, u32[]{:S(2)}) %collective-permute-start.3) | collective-permute-done | bytes 16416 | tf_op jit(solution)/shard_map/ppermute | solution.py:334
  117.8 0.0 collective-permute-done.4
  117.8 0.0 collective-permute-done.5
  117.9 0.0 collective-permute-done.6
  117.9 1.6 collective-permute-start.7
  119.5 0.1 pad_add_fusion.spot_ref
  119.6 0.8 collective-permute-done.7.theirs_ref
  120.4 0.0 all-to-all-done
  120.4 0.0 copy-done.3
  120.4 11.6 %attend.1 = bf16[8,256,1024]{2,1,0:T(8,128)(2,1)S(1)} custom-call(bf16[8,256,1024]{2,1,0:T(8,128)(2,1)} %bitcast.4.arrived_ref, bf16[4,8,256]{2,1,0:T(8,128)(2,1)S(1)} %constant_dynamic-update-slice_fusion.near_ref, bf16[16,8,256]{2,1,0:T(8,128)(2,1)S(1)} %constant_dynamic-update-slice_fusion.4.mine_ref, ...), custom_call_target="tpu_custom_call" | custom-call | tf_op jit(solution)/shard_map/attend/pallas_call | solution.py:386
  132.0 0.0 copy-start
  132.0 0.0 copy-start.1
  132.0 0.0 copy-start.2
  132.1 0.0 copy-start.4
  132.1 0.0 copy-start.5
  132.1 0.0 copy-start.6
  132.1 106.1 %all_to_all.10 = bf16[256,8,1024]{2,1,0:T(8,128)(2,1)S(1)} all-to-all(bf16[256,8,1024]{2,1,0:T(8,128)(2,1)S(1)} %bitcast.14), channel_id=1, replica_groups=mesh['dp'=32,'grp'=8] {'grp','dp'}, dimensions={0} | all-to-all | bytes 8388608 | tf_op jit(solution)/shard_map/all_to_all | solution.py:380
  238.2 0.0 copy-done
  238.2 0.0 copy-done.1
  238.2 0.0 copy-done.2
  238.2 0.0 copy-done.4
  238.2 0.0 copy-done.5
  238.2 0.0 copy-done.6
  238.2 3.3 %unpack.1 = (bf16[128,2048]{1,0:T(8,128)(2,1)}, bf16[128,2048]{1,0:T(8,128)(2,1)}, bf16[128,2048]{1,0:T(8,128)(2,1)}, bf16[128,2048]{1,0:T(8,128)(2,1)}) custom-call(bf16[8,256,1024]{2,1,0:T(8,128)(2,1)S(1)} %bitcast.15, bf16[128,2048]{1,0:T(8,128)(2,1)S(1)} %copy-done, bf16[128,2048]{1,0:T(8,128)(2,1)S(1)} %copy-done.1, f32[1,128]{1,0:T(1,128)S(1)} %bitcast.17, ...), custom_call_target="tpu_custom_call" | custom-call | tf_op jit(solution)/shard_map/unpack/pallas_call | solution.py:408
  (9 shorter events, 0.0 us)
Async XLA Ops:
  6.4 16.7 %copy-start.7 = (bf16[8,128]{1,0:T(8,128)(2,1)S(1)}, bf16[8,128]{1,0:T(8,128)(2,1)}, u32[]{:S(2)}) copy-start(bf16[8,128]{1,0:T(8,128)(2,1)} %get-tuple-element.7) | copy-start | bytes 6148
  6.4 114.0 %copy-start.3 = (s32[1,1024]{1,0:T(1,128)S(1)}, s32[1,1024]{1,0:T(1,128)}, u32[]{:S(2)}) copy-start(s32[1,1024]{1,0:T(1,128)} %clip_ref.1) | copy-start | bytes 12292
  6.4 114.0 %all-to-all-start = ((bf16[256,8,1024]{2,1,0:T(8,128)(2,1)}), bf16[256,8,1024]{2,1,0:T(8,128)(2,1)}, u32[]{:S(2)}, u32[]{:S(2)}) async-start(bf16[256,8,1024]{2,1,0:T(8,128)(2,1)} %bitcast.22), calls=%async_computation | async-start | bytes 8388608 | tf_op jit(solution)/shard_map/all_to_all | solution.py:380
  38.6 6.6 %collective-permute-start.2 = (bf16[1,8,256]{2,1,0:T(8,128)(2,1)S(1)}, bf16[1,8,256]{2,1,0:T(8,128)(2,1)S(1)}, u32[]{:S(2)}, u32[]{:S(2)}) collective-permute-start(bf16[1,8,256]{2,1,0:T(8,128)(2,1)S(1)} %reshape.37), channel_id=1, source_target_pairs={{0,192},{8,200},{16,208},{24,216},{32,224},{40,232},{48,240},{56,2... | collective-permute-start | bytes 12296 | tf_op jit(solution)/shard_map/ppermute | solution.py:321
  40.7 4.5 %collective-permute-start.1 = (bf16[1,8,256]{2,1,0:T(8,128)(2,1)S(1)}, bf16[1,8,256]{2,1,0:T(8,128)(2,1)S(1)}, u32[]{:S(2)}, u32[]{:S(2)}) collective-permute-start(bf16[1,8,256]{2,1,0:T(8,128)(2,1)S(1)} %reshape.37), channel_id=1, source_target_pairs={{0,128},{8,136},{16,144},{24,152},{32,160},{40,168},{48,176},{56,1... | collective-permute-start | bytes 12296 | tf_op jit(solution)/shard_map/ppermute | solution.py:321
  41.1 4.1 %collective-permute-start = (bf16[1,8,256]{2,1,0:T(8,128)(2,1)S(1)}, bf16[1,8,256]{2,1,0:T(8,128)(2,1)S(1)}, u32[]{:S(2)}, u32[]{:S(2)}) collective-permute-start(bf16[1,8,256]{2,1,0:T(8,128)(2,1)S(1)} %reshape.37), channel_id=1, source_target_pairs={{0,64},{8,72},{16,80},{24,88},{32,96},{40,104},{48,112},{56,120},{... | collective-permute-start | bytes 12296 | tf_op jit(solution)/shard_map/ppermute | solution.py:321
  45.2 72.7 %collective-permute-start.3 = (bf16[4,8,256]{2,1,0:T(8,128)(2,1)S(1)}, bf16[4,8,256]{2,1,0:T(8,128)(2,1)S(1)}, u32[]{:S(2)}, u32[]{:S(2)}) collective-permute-start(bf16[4,8,256]{2,1,0:T(8,128)(2,1)S(1)} %constant_dynamic-update-slice_fusion.near_ref), channel_id=1, source_target_pairs={{0,8},{1,33},{2,10},{3,35},{4,12},{5,37},{6,14},{7,39},{8,16},{9,4... | collective-permute-start | bytes 49160 | tf_op jit(solution)/shard_map/ppermute | solution.py:334
  53.7 64.2 %collective-permute-start.6 = (bf16[4,8,256]{2,1,0:T(8,128)(2,1)S(1)}, bf16[4,8,256]{2,1,0:T(8,128)(2,1)S(1)}, u32[]{:S(2)}, u32[]{:S(2)}) collective-permute-start(bf16[4,8,256]{2,1,0:T(8,128)(2,1)S(1)} %constant_dynamic-update-slice_fusion.near_ref), channel_id=1, source_target_pairs={{0,32},{1,57},{2,34},{3,59},{4,36},{5,61},{6,38},{7,63},{8,40},{9,... | collective-permute-start | bytes 49160 | tf_op jit(solution)/shard_map/ppermute | solution.py:334
  53.7 64.2 %collective-permute-start.5 = (bf16[4,8,256]{2,1,0:T(8,128)(2,1)S(1)}, bf16[4,8,256]{2,1,0:T(8,128)(2,1)S(1)}, u32[]{:S(2)}, u32[]{:S(2)}) collective-permute-start(bf16[4,8,256]{2,1,0:T(8,128)(2,1)S(1)} %constant_dynamic-update-slice_fusion.near_ref), channel_id=1, source_target_pairs={{0,24},{1,49},{2,26},{3,51},{4,28},{5,53},{6,30},{7,55},{8,32},{9,... | collective-permute-start | bytes 49160 | tf_op jit(solution)/shard_map/ppermute | solution.py:334
  53.7 64.1 %collective-permute-start.4 = (bf16[4,8,256]{2,1,0:T(8,128)(2,1)S(1)}, bf16[4,8,256]{2,1,0:T(8,128)(2,1)S(1)}, u32[]{:S(2)}, u32[]{:S(2)}) collective-permute-start(bf16[4,8,256]{2,1,0:T(8,128)(2,1)S(1)} %constant_dynamic-update-slice_fusion.near_ref), channel_id=1, source_target_pairs={{0,16},{1,41},{2,18},{3,43},{4,20},{5,45},{6,22},{7,47},{8,24},{9,... | collective-permute-start | bytes 49160 | tf_op jit(solution)/shard_map/ppermute | solution.py:334
  117.9 2.5 %collective-permute-start.7 = (bf16[16,8,256]{2,1,0:T(8,128)(2,1)S(1)}, bf16[16,8,256]{2,1,0:T(8,128)(2,1)S(1)}, u32[]{:S(2)}, u32[]{:S(2)}) collective-permute-start(bf16[16,8,256]{2,1,0:T(8,128)(2,1)S(1)} %constant_dynamic-update-slice_fusion.4.mine_ref), channel_id=1, source_target_pairs={{0,1},{1,0},{2,3},{3,2},{4,5},{5,4},{6,7},{7,6},{8,9},{9,8},{10,11... | collective-permute-start | bytes 196616 | tf_op jit(solution)/shard_map/ppermute | solution.py:337
  132.0 106.2 %copy-start = (bf16[128,2048]{1,0:T(8,128)(2,1)S(1)}, bf16[128,2048]{1,0:T(8,128)(2,1)}, u32[]{:S(2)}) copy-start(bf16[128,2048]{1,0:T(8,128)(2,1)} %query_ref.1) | copy-start | bytes 1572868
  132.0 106.2 %copy-start.1 = (bf16[128,2048]{1,0:T(8,128)(2,1)S(1)}, bf16[128,2048]{1,0:T(8,128)(2,1)}, u32[]{:S(2)}) copy-start(bf16[128,2048]{1,0:T(8,128)(2,1)} %key_ref.1) | copy-start | bytes 1572868
  132.0 106.1 %copy-start.2 = (s32[3,128]{1,0:T(4,128)S(1)}, s32[3,128]{1,0:T(4,128)}, u32[]{:S(2)}) copy-start(s32[3,128]{1,0:T(4,128)} %positions_ref.1) | copy-start | bytes 4612
  132.1 106.1 %copy-start.4 = (f32[128]{0:T(128)S(1)}, f32[128]{0:T(128)}, u32[]{:S(2)}) copy-start(f32[128]{0:T(128)} %param.13) | copy-start | bytes 1540
  132.1 106.1 %copy-start.5 = (f32[128]{0:T(128)S(1)}, f32[128]{0:T(128)}, u32[]{:S(2)}) copy-start(f32[128]{0:T(128)} %param.14) | copy-start | bytes 1540
  132.1 106.1 %copy-start.6 = (s32[128]{0:T(128)S(1)}, s32[128]{0:T(128)}, u32[]{:S(2)}) copy-start(s32[128]{0:T(128)} %param.16) | copy-start | bytes 1540

commit v3 on v2

--- a/solution.py
+++ b/solution.py
@@ -106,7 +106,7 @@
     code = jnp.where(rank, ((place & (n - 1)) + 1).astype(jnp.float32), 0.0).astype(jnp.bfloat16)
     target = lax.broadcasted_iota(jnp.int32, (n, n), 0) == (slot // CAP)
     target = jnp.where(target, 1.0, 0.0).astype(jnp.bfloat16)
-    code_ref[...] = f32_dot(code, target, ((1,), (1,))).astype(jnp.bfloat16)
+    code_ref[...] = f32_dot(code, target, ((1,), (1,)))
     copies[6].wait()
     cosine, sine = rotation(positions_ref[...])
     swap = swap_matrix(narrow)
@@ -152,8 +152,6 @@
     pick_ref,
     query_clip_ref,
     key_clip_ref,
-    weights_ref,
-    scores_ref,
     by_query_ref,
     by_key_ref,
 ):
@@ -161,31 +159,30 @@
     rows, columns = token_ref.shape
     width = columns // 4
     own = rows // grp_count
-    block = rows // 4
     bf16 = jnp.bfloat16
 
     here, core = spot_ref[0], spot_ref[1]
     half = Z_COUNT // 2
     here_y, here_z = here // Z_COUNT, here & (Z_COUNT - 1)
 
-    def put_codes(ref, entry, back_z, back_y):
-        source_y = (here_y - back_y) & (Y_COUNT - 1)
+    steps = lax.broadcasted_iota(jnp.int32, (CAP, code_ref.shape[1]), 1) // grp_count
+
+    def put_codes(codes, back_z):
         source_z = (here_z - back_z) & (Z_COUNT - 1)
-        start = pl.multiple_of((source_y * Z_COUNT + source_z) * CAP, CAP)
-        code_ref[pl.ds(start, CAP), :] = ref[entry].astype(jnp.float32)
-
-    for back_y in range(Y_COUNT):
-        put_codes(near_ref, back_y, 0, back_y)
-        for step in range(1, half + 1):
-            entry = (step - 1) * Y_COUNT + back_y
-            put_codes(mine_ref, entry, step + (half - 1) * core, back_y)
-            put_codes(theirs_ref, entry, step + (half - 1) * (1 - core), back_y)
-
-    dp_count = slots // CAP
+        for back_y in range(Y_COUNT):
+            source_y = (here_y - back_y) & (Y_COUNT - 1)
+            start = pl.multiple_of((source_y * Z_COUNT + source_z) * CAP, CAP)
+            code_ref[pl.ds(start, CAP), :] = jnp.where(steps == back_y, codes, 0.0)
+
+    put_codes(near_ref[0], 0)
+    for step in range(1, half + 1):
+        put_codes(mine_ref[step - 1], step + (half - 1) * core)
+        put_codes(theirs_ref[step - 1], step + (half - 1) * (1 - core))
+
     codes = code_ref[...].astype(bf16)
-    lane = lax.broadcasted_iota(jnp.int32, (rows, slots), 1)
-    grp = lax.broadcasted_iota(jnp.int32, (rows, slots), 0) // own
-    chosen = jnp.where(lane == grp * dp_count + here, 1.0, 0.0).astype(bf16)
+    shape = (rows, codes.shape[1])
+    lane = lax.broadcasted_iota(jnp.int32, shape, 1) & (grp_count - 1)
+    chosen = jnp.where(lane == lax.broadcasted_iota(jnp.int32, shape, 0) // own, 1.0, 0.0).astype(bf16)
     by_slot = f32_dot(codes, chosen, ((1,), (1,)))
     by_place = f32_dot(chosen, codes, ((1,), (1,)))
     across = (lax.broadcasted_iota(jnp.int32, (slots, own), 1) + 1).astype(jnp.float32)
@@ -204,47 +201,34 @@
     query_clip_ref[...] = jnp.where(channel == clip, 1.0, 0.0).astype(bf16)
     key_clip_ref[...] = jnp.where(channel == 1 - clip, -4096.0, 0.0).astype(bf16)
 
-    spans = [(0, 3 * block), (0, rows), (0, rows), (block, rows)]
     for head in range(width // HEAD_DIM):
-        at = [slice(a * width + head * HEAD_DIM, a * width + (head + 1) * HEAD_DIM) for a in range(4)]
-        for i, (low, high) in enumerate(spans):
-            part = slice(i * block, (i + 1) * block)
-            query = token_ref[part, at[0]]
-            key = token_ref[low:high, at[1]]
-            value = token_ref[low:high, at[2]]
-            grad = token_ref[part, at[3]]
-            scores = f32_dot(
-                jnp.concatenate([query, query_clip_ref[part, :]], axis=1),
-                jnp.concatenate([key, key_clip_ref[low:high, :]], axis=1),
-                ((1,), (1,)),
-            )
-            raised = jnp.exp2(scores * (factor * math.log2(math.e)))
-            weights = raised * (1.0 / jnp.sum(raised, axis=1, keepdims=True))
-            weights_low = weights.astype(bf16)
-            weights_ref[part, low:high] = weights_low
-            attended = f32_dot(weights_low, value, ((1,), (0,))).astype(bf16)
-            by_query_ref[part, head * HEAD_DIM : (head + 1) * HEAD_DIM] = attended
-            row_dot = jnp.sum(
-                grad.astype(jnp.float32) * attended.astype(jnp.float32), axis=1, keepdims=True
-            )
-            grad_weights = f32_dot(grad, value, ((1,), (1,)))
-            grad_scores = (weights * (grad_weights - row_dot)).astype(bf16)
-            scores_ref[part, low:high] = grad_scores
-            grad_query = f32_dot(grad_scores, key, ((1,), (0,))) * factor
-            by_query_ref[part, width + head * HEAD_DIM : width + (head + 1) * HEAD_DIM] = (
-                grad_query.astype(bf16)
-            )
-        meets = [(0, block, 0, 3 * block), (block, 3 * block, 0, rows), (3 * block, rows, block, rows)]
-        for low, high, first, last in meets:
-            query = token_ref[first:last, at[0]]
-            grad = token_ref[first:last, at[3]]
-            channels = slice(head * HEAD_DIM, (head + 1) * HEAD_DIM)
-            by_key_ref[0, channels, low:high] = (
-                f32_dot(query, scores_ref[first:last, low:high], ((0,), (0,))) * factor
-            ).astype(bf16)
-            by_key_ref[1, channels, low:high] = f32_dot(
-                grad, weights_ref[first:last, low:high], ((0,), (0,))
-            ).astype(bf16)
+        channels = slice(head * HEAD_DIM, (head + 1) * HEAD_DIM)
+        query, key, value, grad = [
+            token_ref[:, a * width + head * HEAD_DIM : a * width + (head + 1) * HEAD_DIM]
+            for a in range(4)
+        ]
+        scores = f32_dot(
+            jnp.concatenate([query, query_clip_ref[...]], axis=1),
+            jnp.concatenate([key, key_clip_ref[...]], axis=1),
+            ((1,), (1,)),
+        )
+        raised = jnp.exp2(scores * (factor * math.log2(math.e)))
+        weights = raised * (1.0 / jnp.sum(raised, axis=1, keepdims=True))
+        weights_low = weights.astype(bf16)
+        attended = f32_dot(weights_low, value, ((1,), (0,))).astype(bf16)
+        by_query_ref[:, channels] = attended
+        row_dot = jnp.sum(
+            grad.astype(jnp.float32) * attended.astype(jnp.float32), axis=1, keepdims=True
+        )
+        grad_weights = f32_dot(grad, value, ((1,), (1,)))
+        grad_scores = (weights * (grad_weights - row_dot)).astype(bf16)
+        grad_query = f32_dot(grad_scores, key, ((1,), (0,))) * factor
+        by_query_ref[:, width + head * HEAD_DIM : width + (head + 1) * HEAD_DIM] = (
+            grad_query.astype(bf16)
+        )
+        grad_key = f32_dot(query, grad_scores, ((0,), (0,))) * factor
+        by_key_ref[0, channels, :] = grad_key.astype(bf16)
+        by_key_ref[1, channels, :] = f32_dot(grad, weights_low, ((0,), (0,))).astype(bf16)
 
     for g in range(grp_count):
         pick = pick_ref[g]
@@ -312,16 +296,24 @@
 
 def gather_codes(codes):
     grp_count = lax.axis_size("grp")
+    dp_index = lax.axis_index("dp")
+    core = lax.axis_index("grp") % 2
     here = lax.all_gather(codes, "grp", axis=0)
-    here = jnp.transpose(here, (1, 0, 2)).reshape(1, codes.shape[0], -1)
     spots = [(y, z) for y in range(Y_COUNT) for z in range(Z_COUNT)]
 
     def y_step(step):
         pairs = [(y * Z_COUNT + z, (y + step) % Y_COUNT * Z_COUNT + z) for y, z in spots]
         return lax.ppermute(here, "dp", pairs)
 
-    near = jnp.concatenate([here] + [y_step(step) for step in range(1, Y_COUNT)], axis=0)
+    along_y = jnp.stack([here] + [y_step(step) for step in range(1, Y_COUNT)])
+    along_y = along_y.reshape(Y_COUNT, grp_count, CAP, Y_COUNT, Z_COUNT)
+    along_y = lax.dynamic_index_in_dim(along_y, dp_index // Z_COUNT, axis=3, keepdims=False)
+    by_target = jnp.transpose(along_y, (3, 2, 0, 1)).reshape(Z_COUNT, CAP, Y_COUNT * grp_count)
     half = Z_COUNT // 2
+
+    def for_step(step):
+        target = (dp_index + step) % Z_COUNT
+        return lax.dynamic_slice_in_dim(by_target, target, 1, axis=0)
 
     def z_step(step):
         pairs = []
@@ -331,11 +323,11 @@
                 pairs.append(
                     ((y * Z_COUNT + z) * grp_count + grp, (y * Z_COUNT + target) * grp_count + grp)
                 )
-        return lax.ppermute(near, ("dp", "grp"), pairs)
+        return lax.ppermute(for_step(step + (half - 1) * core), ("dp", "grp"), pairs)
 
     mine = jnp.concatenate([z_step(step) for step in range(1, half + 1)], axis=0)
     theirs = lax.ppermute(mine, "grp", [(grp, grp ^ 1) for grp in range(grp_count)])
-    return near, mine, theirs
+    return for_step(0), mine, theirs
 
 
 def on_device(
@@ -363,7 +355,7 @@
         out_specs=[in_hbm, pl.BlockSpec(memory_space=pltpu.VMEM)],
         out_shape=[
             jax.ShapeDtypeStruct(sent_shape, bf16),
-            jax.ShapeDtypeStruct((CAP, n), bf16),
+            jax.ShapeDtypeStruct((CAP, n), jnp.float32),
         ],
         scratch_shapes=[vmem(a.shape, a.dtype) for a in arguments]
         + [
@@ -390,13 +382,11 @@
         + [pl.BlockSpec(memory_space=pltpu.SMEM), pl.BlockSpec(memory_space=pltpu.VMEM)],
         out_shape=jax.ShapeDtypeStruct((grp_count, slots, 4 * narrow), bf16),
         scratch_shapes=[
-            vmem((slots, slots), jnp.float32),
+            vmem((slots, near.shape[2]), jnp.float32),
             vmem((group_rows, 4 * narrow), bf16),
             vmem((grp_count, slots, n), bf16),
             vmem((group_rows, HEAD_DIM), bf16),
             vmem((group_rows, HEAD_DIM), bf16),
-            vmem((group_rows, group_rows), bf16),
-            vmem((group_rows, group_rows), bf16),
             vmem((group_rows, 2 * narrow), bf16),
             vmem((2, narrow, group_rows), bf16),
         ],

time: 242 us -> 240 us (level)
    ppermute x4, waiting for transfers between devices: 60 us -> 56.5 us  [z_step(): lax.ppermute(for_step(step + (half - 1) * core), ('dp', 'grp'), pairs)]
  transfers between devices with their start and end apart: 9 -> 9, of which waited for: 3 -> 5; matrix products, arithmetic and copies ran while one was open for 0% -> 0% of each run, Pallas kernels for 0% -> 0%
where the time goes in v3:
time: 240 us; the launch traced here: 239 us
  blocking collectives  122 us (51%)
  waiting for transfers between devices  62.2 us (26%)
  starting transfers between devices  33.4 us (14%)
  Pallas kernels  19.6 us (8%)
    all_to_all x1, blocking collectives, exchange(): lax.all_to_all(flat, ('grp', 'dp'), split_axis=0, concat_axis=0, tiled=True)  105 us
    ppermute x4, waiting for transfers between devices, z_step(): lax.ppermute(for_step(step + (half - 1) * core), ('dp', 'grp'), pairs)  56.5 us
    all_gather x1, blocking collectives, gather_codes(): here = lax.all_gather(codes, 'grp', axis=0)  17 us
    all_to_all x1, starting transfers between devices, exchange(): lax.all_to_all(flat, ('grp', 'dp'), split_axis=0, concat_axis=0, tiled=True)  16.7 us
    ppermute x4, starting transfers between devices, z_step(): lax.ppermute(for_step(step + (half - 1) * core), ('dp', 'grp'), pairs)  12.7 us
    pallas_call x1, Pallas kernels, on_device(): pl.pallas_call(attend_kernel, name='attend', in_specs=[pl.BlockSpec(memor...  10.6 us
    pallas_call x1, Pallas kernels, on_device(): pl.pallas_call(functools.partial(pack_kernel, group_rows), name='pack', i...  5.75 us
  transfers between devices with their start and end apart: 9, of which 5 were waited for; matrix products, arithmetic and copies ran while one was open for 0% of the time, Pallas kernels for 0%

profile of v3, /device:TPU:1, one launch (start us, length us, event | category | flops | bytes accessed | tf_op | source)
XLA Modules:
  0.0 239.2 jit_solution(8960685436481564855)
XLA Ops:
  0.6 5.8 %pack.1 = (bf16[8,256,1024]{2,1,0:T(8,128)(2,1)}, f32[8,128]{1,0:T(8,128)}) custom-call(bf16[128,2048]{1,0:T(8,128)(2,1)} %query_ref.1, bf16[128,2048]{1,0:T(8,128)(2,1)} %key_ref.1, bf16[128,2048]{1,0:T(8,128)(2,1)} %refs_2_.1, bf16[128,2048]{1,0:T(8,128)(2,1)} %refs_3_.1, f32[1,128]{1,0:T(1,128)} %bitcast.22, f32[1,128]{1,0:T(1,128)} %bitcast.24, ...), custom_call_target="tpu_custom_call" | custom-call | tf_op jit(solution)/shard_map/pack/pallas_call | solution.py:351
  6.4 0.0 copy-start.7
  6.4 0.0 copy-start.3
  6.4 16.7 %all-to-all-start = ((bf16[256,8,1024]{2,1,0:T(8,128)(2,1)}), bf16[256,8,1024]{2,1,0:T(8,128)(2,1)}, u32[]{:S(2)}, u32[]{:S(2)}) async-start(bf16[256,8,1024]{2,1,0:T(8,128)(2,1)} %bitcast.28), calls=%async_computation | async-start | bytes 8388608 | tf_op jit(solution)/shard_map/all_to_all | solution.py:372
  23.1 0.0 copy-done.7
  23.1 17.0 %all-gather = f32[64,32]{1,0:T(8,128)S(1)} all-gather(f32[8,32]{1,0:T(8,128)S(1)} %bitcast.35), channel_id=2, replica_groups=mesh['dp'=32,'grp'=8] {'grp'}, dimensions={0}, use_global_device_ids=true | all-gather | bytes 9216 | tf_op jit(solution)/shard_map/all_gather | solution.py:301
  40.1 2.0 collective-permute-start.2
  42.1 0.0 collective-permute-start
  42.1 1.4 collective-permute-start.1
  43.6 0.1 copy.18
  43.6 0.1 stack.24
  43.8 0.2 collective-permute-done.2
  44.0 0.1 copy.21
  44.1 3.9 %collective-permute-done = f32[8,8,32]{2,1,0:T(8,128)S(1)} collective-permute-done((f32[8,8,32]{2,1,0:T(8,128)S(1)}, f32[8,8,32]{2,1,0:T(8,128)S(1)}, u32[]{:S(2)}, u32[]{:S(2)}) %collective-permute-start) | collective-permute-done | bytes 8224 | tf_op jit(solution)/shard_map/ppermute | solution.py:306
  48.1 0.1 copy.19
  48.2 0.0 collective-permute-done.1
  48.2 0.1 copy.20
  48.3 0.1 copy.23
  48.4 0.1 reshape.46
  48.6 7.6 %collective-permute-start.3 = (f32[1,8,32]{2,1,0:T(8,128)S(1)}, f32[1,8,32]{2,1,0:T(8,128)S(1)}, u32[]{:S(2)}, u32[]{:S(2)}) collective-permute-start(f32[1,8,32]{2,1,0:T(8,128)S(1)} %get-tuple-element.11), channel_id=1, source_target_pairs={{0,8},{1,33},{2,10},{3,35},{4,12},{5,37},{6,14},{7,39},{8,16},{9,4... | collective-permute-start | bytes 3080 | tf_op jit(solution)/shard_map/ppermute | solution.py:326
  56.2 0.2 collective-permute-start.6
  56.4 0.7 collective-permute-start.5
  57.1 4.2 %collective-permute-start.4 = (f32[1,8,32]{2,1,0:T(8,128)S(1)}, f32[1,8,32]{2,1,0:T(8,128)S(1)}, u32[]{:S(2)}, u32[]{:S(2)}) collective-permute-start(f32[1,8,32]{2,1,0:T(8,128)S(1)} %get-tuple-element.10), channel_id=1, source_target_pairs={{0,16},{1,41},{2,18},{3,43},{4,20},{5,45},{6,22},{7,47},{8,24},{9,... | collective-permute-start | bytes 3080 | tf_op jit(solution)/shard_map/ppermute | solution.py:326
  61.3 56.5 %collective-permute-done.3 = f32[1,8,32]{2,1,0:T(8,128)S(1)} collective-permute-done((f32[1,8,32]{2,1,0:T(8,128)S(1)}, f32[1,8,32]{2,1,0:T(8,128)S(1)}, u32[]{:S(2)}, u32[]{:S(2)}) %collective-permute-start.3) | collective-permute-done | bytes 1056 | tf_op jit(solution)/shard_map/ppermute | solution.py:326
  117.8 0.0 collective-permute-done.4
  117.8 0.0 collective-permute-done.5
  117.8 0.0 collective-permute-done.6
  117.8 0.6 collective-permute-start.7
  118.4 0.1 pad_add_fusion.spot_ref
  118.5 0.8 collective-permute-done.7.theirs_ref
  119.3 0.7 all-to-all-done
  120.0 0.0 copy-done.3
  120.0 10.6 %attend.1 = bf16[8,256,1024]{2,1,0:T(8,128)(2,1)S(1)} custom-call(bf16[8,256,1024]{2,1,0:T(8,128)(2,1)} %bitcast.4.arrived_ref, f32[1,8,32]{2,1,0:T(8,128)S(1)} %get-tuple-element.12.near_ref, f32[4,8,32]{2,1,0:T(8,128)S(1)} %constant_dynamic-update-slice_fusion.mine_ref, f32[4,8,32]{2,1,0:T(8,128)S(1)} %collective-permute-done.7.theirs_ref, ...), custom_call_target="tpu_custom_call" | custom-call | tf_op jit(solution)/shard_map/attend/pallas_call | solution.py:378
  130.6 0.0 copy-start
  130.6 0.0 copy-start.1
  130.6 0.0 copy-start.2
  130.6 0.0 copy-start.4
  130.6 0.0 copy-start.5
  130.6 0.0 copy-start.6
  130.6 105.1 %all_to_all.10 = bf16[256,8,1024]{2,1,0:T(8,128)(2,1)S(1)} all-to-all(bf16[256,8,1024]{2,1,0:T(8,128)(2,1)S(1)} %bitcast.20), channel_id=1, replica_groups=mesh['dp'=32,'grp'=8] {'grp','dp'}, dimensions={0} | all-to-all | bytes 8388608 | tf_op jit(solution)/shard_map/all_to_all | solution.py:372
  235.7 0.0 copy-done
  235.7 0.0 copy-done.1
  235.7 0.0 copy-done.2
  235.7 0.0 copy-done.4
  235.8 0.0 copy-done.5
  235.8 0.0 copy-done.6
  235.8 3.3 %unpack.1 = (bf16[128,2048]{1,0:T(8,128)(2,1)}, bf16[128,2048]{1,0:T(8,128)(2,1)}, bf16[128,2048]{1,0:T(8,128)(2,1)}, bf16[128,2048]{1,0:T(8,128)(2,1)}) custom-call(bf16[8,256,1024]{2,1,0:T(8,128)(2,1)S(1)} %bitcast.21, bf16[128,2048]{1,0:T(8,128)(2,1)S(1)} %copy-done, bf16[128,2048]{1,0:T(8,128)(2,1)S(1)} %copy-done.1, f32[1,128]{1,0:T(1,128)S(1)} %bitcast.23, ...), custom_call_target="tpu_custom_call" | custom-call | tf_op jit(solution)/shard_map/unpack/pallas_call | solution.py:398
  (6 shorter events, 0.0 us)
Async XLA Ops:
  6.4 16.7 %copy-start.7 = (f32[8,128]{1,0:T(8,128)S(1)}, f32[8,128]{1,0:T(8,128)}, u32[]{:S(2)}) copy-start(f32[8,128]{1,0:T(8,128)} %get-tuple-element.7) | copy-start | bytes 12292
  6.4 113.6 %copy-start.3 = (s32[1,1024]{1,0:T(1,128)S(1)}, s32[1,1024]{1,0:T(1,128)}, u32[]{:S(2)}) copy-start(s32[1,1024]{1,0:T(1,128)} %clip_ref.1) | copy-start | bytes 12292
  6.4 113.6 %all-to-all-start = ((bf16[256,8,1024]{2,1,0:T(8,128)(2,1)}), bf16[256,8,1024]{2,1,0:T(8,128)(2,1)}, u32[]{:S(2)}, u32[]{:S(2)}) async-start(bf16[256,8,1024]{2,1,0:T(8,128)(2,1)} %bitcast.28), calls=%async_computation | async-start | bytes 8388608 | tf_op jit(solution)/shard_map/all_to_all | solution.py:372
  40.1 3.9 %collective-permute-start.2 = (f32[8,8,32]{2,1,0:T(8,128)S(1)}, f32[8,8,32]{2,1,0:T(8,128)S(1)}, u32[]{:S(2)}, u32[]{:S(2)}) collective-permute-start(f32[8,8,32]{2,1,0:T(8,128)S(1)} %bitcast.32), channel_id=1, source_target_pairs={{0,192},{8,200},{16,208},{24,216},{32,224},{40,232},{48,240},{56,2... | collective-permute-start | bytes 24584 | tf_op jit(solution)/shard_map/ppermute | solution.py:306
  42.1 5.9 %collective-permute-start = (f32[8,8,32]{2,1,0:T(8,128)S(1)}, f32[8,8,32]{2,1,0:T(8,128)S(1)}, u32[]{:S(2)}, u32[]{:S(2)}) collective-permute-start(f32[8,8,32]{2,1,0:T(8,128)S(1)} %bitcast.33), channel_id=1, source_target_pairs={{0,64},{8,72},{16,80},{24,88},{32,96},{40,104},{48,112},{56,120},{... | collective-permute-start | bytes 24584 | tf_op jit(solution)/shard_map/ppermute | solution.py:306
  42.1 6.1 %collective-permute-start.1 = (f32[8,8,32]{2,1,0:T(8,128)S(1)}, f32[8,8,32]{2,1,0:T(8,128)S(1)}, u32[]{:S(2)}, u32[]{:S(2)}) collective-permute-start(f32[8,8,32]{2,1,0:T(8,128)S(1)} %bitcast.34), channel_id=1, source_target_pairs={{0,128},{8,136},{16,144},{24,152},{32,160},{40,168},{48,176},{56,1... | collective-permute-start | bytes 24584 | tf_op jit(solution)/shard_map/ppermute | solution.py:306
  48.6 69.2 %collective-permute-start.3 = (f32[1,8,32]{2,1,0:T(8,128)S(1)}, f32[1,8,32]{2,1,0:T(8,128)S(1)}, u32[]{:S(2)}, u32[]{:S(2)}) collective-permute-start(f32[1,8,32]{2,1,0:T(8,128)S(1)} %get-tuple-element.11), channel_id=1, source_target_pairs={{0,8},{1,33},{2,10},{3,35},{4,12},{5,37},{6,14},{7,39},{8,16},{9,4... | collective-permute-start | bytes 3080 | tf_op jit(solution)/shard_map/ppermute | solution.py:326
  56.2 61.6 %collective-permute-start.6 = (f32[1,8,32]{2,1,0:T(8,128)S(1)}, f32[1,8,32]{2,1,0:T(8,128)S(1)}, u32[]{:S(2)}, u32[]{:S(2)}) collective-permute-start(f32[1,8,32]{2,1,0:T(8,128)S(1)} %get-tuple-element.8), channel_id=1, source_target_pairs={{0,32},{1,57},{2,34},{3,59},{4,36},{5,61},{6,38},{7,63},{8,40},{9,... | collective-permute-start | bytes 3080 | tf_op jit(solution)/shard_map/ppermute | solution.py:326
  56.4 61.4 %collective-permute-start.5 = (f32[1,8,32]{2,1,0:T(8,128)S(1)}, f32[1,8,32]{2,1,0:T(8,128)S(1)}, u32[]{:S(2)}, u32[]{:S(2)}) collective-permute-start(f32[1,8,32]{2,1,0:T(8,128)S(1)} %get-tuple-element.9), channel_id=1, source_target_pairs={{0,24},{1,49},{2,26},{3,51},{4,28},{5,53},{6,30},{7,55},{8,32},{9,... | collective-permute-start | bytes 3080 | tf_op jit(solution)/shard_map/ppermute | solution.py:326
  57.1 60.7 %collective-permute-start.4 = (f32[1,8,32]{2,1,0:T(8,128)S(1)}, f32[1,8,32]{2,1,0:T(8,128)S(1)}, u32[]{:S(2)}, u32[]{:S(2)}) collective-permute-start(f32[1,8,32]{2,1,0:T(8,128)S(1)} %get-tuple-element.10), channel_id=1, source_target_pairs={{0,16},{1,41},{2,18},{3,43},{4,20},{5,45},{6,22},{7,47},{8,24},{9,... | collective-permute-start | bytes 3080 | tf_op jit(solution)/shard_map/ppermute | solution.py:326
  117.8 1.5 collective-permute-start.7
  130.6 105.2 %copy-start = (bf16[128,2048]{1,0:T(8,128)(2,1)S(1)}, bf16[128,2048]{1,0:T(8,128)(2,1)}, u32[]{:S(2)}) copy-start(bf16[128,2048]{1,0:T(8,128)(2,1)} %query_ref.1) | copy-start | bytes 1572868
  130.6 105.2 %copy-start.1 = (bf16[128,2048]{1,0:T(8,128)(2,1)S(1)}, bf16[128,2048]{1,0:T(8,128)(2,1)}, u32[]{:S(2)}) copy-start(bf16[128,2048]{1,0:T(8,128)(2,1)} %key_ref.1) | copy-start | bytes 1572868
  130.6 105.2 %copy-start.2 = (s32[3,128]{1,0:T(4,128)S(1)}, s32[3,128]{1,0:T(4,128)}, u32[]{:S(2)}) copy-start(s32[3,128]{1,0:T(4,128)} %positions_ref.1) | copy-start | bytes 4612
  130.6 105.1 %copy-start.4 = (f32[128]{0:T(128)S(1)}, f32[128]{0:T(128)}, u32[]{:S(2)}) copy-start(f32[128]{0:T(128)} %param.13) | copy-start | bytes 1540
  130.6 105.1 %copy-start.5 = (f32[128]{0:T(128)S(1)}, f32[128]{0:T(128)}, u32[]{:S(2)}) copy-start(f32[128]{0:T(128)} %param.14) | copy-start | bytes 1540
  130.6 105.1 %copy-start.6 = (s32[128]{0:T(128)S(1)}, s32[128]{0:T(128)}, u32[]{:S(2)}) copy-start(s32[128]{0:T(128)} %param.16) | copy-start | bytes 1540

commit v4 on v3

--- a/solution.py
+++ b/solution.py
@@ -122,7 +122,7 @@
     sends = []
     for h in range(grp_count):
         block = slice(h * narrow, (h + 1) * narrow)
-        parts = []
+        prepared = []
         for ref, (along, across) in zip((query_ref, key_ref), turns):
             rows = ref[:, block]
             other = f32_dot(rows, swap, ((1,), (0,)))
@@ -130,8 +130,12 @@
                 lanes = slice(start, start + HEAD_DIM)
                 values = rows[:, lanes].astype(jnp.float32)
                 rotated = (values * along + other[:, lanes] * across) * norm_factor(values)
-                parts.append(rotated.astype(jnp.bfloat16))
-        rows = jnp.concatenate(parts + [value_ref[:, block], grad_ref[:, block]], axis=1)
+                prepared.append(rotated.astype(jnp.bfloat16))
+        parts = []
+        for head, start in enumerate(range(h * narrow, (h + 1) * narrow, HEAD_DIM)):
+            lanes = slice(start, start + HEAD_DIM)
+            parts += prepared[head :: narrow // HEAD_DIM] + [value_ref[:, lanes], grad_ref[:, lanes]]
+        rows = jnp.concatenate(parts, axis=1)
         sent_ref[h] = f32_dot(pick_ref[...], rows, ((1,), (0,))).astype(jnp.bfloat16)
         sends.append(pltpu.make_async_copy(sent_ref.at[h], out_ref.at[h], out_sems.at[h]))
         sends[-1].start()
@@ -147,17 +151,31 @@
     spot_ref,
     clip_ref,
     out_ref,
+    slot_ref,
     code_ref,
     token_ref,
     pick_ref,
+    order_ref,
     query_clip_ref,
     key_clip_ref,
     by_query_ref,
     by_key_ref,
+    sems,
 ):
     grp_count, slots, _ = arrived_ref.shape
     rows, columns = token_ref.shape
     width = columns // 4
+    share = 4 * HEAD_DIM
+    heads = columns // share
+    copies = []
+    for head in range(heads):
+        lanes = pl.ds(head * share, share)
+        copies.append(
+            pltpu.make_async_copy(
+                arrived_ref.at[:, :, lanes], slot_ref.at[:, :, lanes], sems.at[head]
+            )
+        )
+    copies[0].start()
     own = rows // grp_count
     bf16 = jnp.bfloat16
 
@@ -191,8 +209,7 @@
     for g in range(grp_count):
         part = slice(g * own, (g + 1) * own)
         pick_ref[g] = jnp.where(by_slot[:, part] == across, 1.0, 0.0).astype(bf16)
-        pick = jnp.where(by_place[part] == down, 1.0, 0.0).astype(bf16)
-        token_ref[part, :] = f32_dot(pick, arrived_ref[g], ((1,), (0,))).astype(bf16)
+        order_ref[g] = jnp.where(by_place[part] == down, 1.0, 0.0).astype(bf16)
 
     first_rows = jnp.sum((clip_ref[...] == 0).astype(jnp.float32), axis=1, keepdims=True)
     place = lax.broadcasted_iota(jnp.int32, (rows, HEAD_DIM), 0).astype(jnp.float32)
@@ -201,10 +218,18 @@
     query_clip_ref[...] = jnp.where(channel == clip, 1.0, 0.0).astype(bf16)
     key_clip_ref[...] = jnp.where(channel == 1 - clip, -4096.0, 0.0).astype(bf16)
 
-    for head in range(width // HEAD_DIM):
+    for head in range(heads):
+        mine = slice(head * share, (head + 1) * share)
+        copies[head].wait()
+        if head + 1 < heads:
+            copies[head + 1].start()
+        for g in range(grp_count):
+            token_ref[g * own : (g + 1) * own, mine] = f32_dot(
+                order_ref[g], slot_ref[g, :, mine], ((1,), (0,))
+            ).astype(bf16)
         channels = slice(head * HEAD_DIM, (head + 1) * HEAD_DIM)
         query, key, value, grad = [
-            token_ref[:, a * width + head * HEAD_DIM : a * width + (head + 1) * HEAD_DIM]
+            token_ref[:, head * share + a * HEAD_DIM : head * share + (a + 1) * HEAD_DIM]
             for a in range(4)
         ]
         scores = f32_dot(
@@ -255,10 +280,14 @@
     grp_count, slots, _ = back_ref.shape
     n, width = query_ref.shape
     narrow = width // grp_count
-    copies = [
-        pltpu.make_async_copy(source, target, sems.at[i])
-        for i, (source, target) in enumerate(zip(held, outs))
-    ]
+    half = grp_count // 2
+
+    def send(index, h):
+        lanes = pl.ds((h // half) * half * narrow, half * narrow)
+        return pltpu.make_async_copy(
+            held[index].at[:, lanes], outs[index].at[:, lanes], sems.at[index, h // half]
+        )
+
     slot = as_column(slot_of_token(place_ref[...], group_rows)).astype(jnp.int32)
     pick = jnp.broadcast_to(slot, (n, slots)) == lax.broadcasted_iota(jnp.int32, (n, slots), 1)
     pick = jnp.where(pick, 1.0, 0.0).astype(jnp.bfloat16)
@@ -270,7 +299,8 @@
     for index, out in ((0, 0), (3, 3)):
         for h in range(grp_count):
             held[out][:, h * narrow : (h + 1) * narrow] = take(h, index).astype(jnp.bfloat16)
-        copies[out].start()
+            if h % half == half - 1:
+                send(out, h).start()
 
     cosine, sine = rotation(positions_ref[...])
     swap = swap_matrix(narrow)
@@ -289,9 +319,11 @@
                 unit = values * scale
                 share = jnp.mean(grad * unit, axis=-1, keepdims=True)
                 held[index][:, lanes] = (scale * (grad - unit * share)).astype(jnp.bfloat16)
-        copies[index].start()
-    for copy in copies:
-        copy.wait()
+            if h % half == half - 1:
+                send(index, h).start()
+    for index in range(4):
+        for h in (0, half):
+            send(index, h).wait()
 
 
 def gather_codes(codes):
@@ -378,17 +410,21 @@
     results = pl.pallas_call(
         attend_kernel,
         name="attend",
-        in_specs=[pl.BlockSpec(memory_space=pltpu.VMEM)] * 4
+        in_specs=[in_hbm]
+        + [pl.BlockSpec(memory_space=pltpu.VMEM)] * 3
         + [pl.BlockSpec(memory_space=pltpu.SMEM), pl.BlockSpec(memory_space=pltpu.VMEM)],
         out_shape=jax.ShapeDtypeStruct((grp_count, slots, 4 * narrow), bf16),
         scratch_shapes=[
+            vmem(sent_shape, bf16),
             vmem((slots, near.shape[2]), jnp.float32),
             vmem((group_rows, 4 * narrow), bf16),
             vmem((grp_count, slots, n), bf16),
+            vmem((grp_count, n, slots), bf16),
             vmem((group_rows, HEAD_DIM), bf16),
             vmem((group_rows, HEAD_DIM), bf16),
             vmem((group_rows, 2 * narrow), bf16),
             vmem((2, narrow, group_rows), bf16),
+            pltpu.SemaphoreType.DMA((narrow // HEAD_DIM,)),
         ],
         compiler_params=pltpu.CompilerParams(vmem_limit_bytes=40 * MB),
     )(arrived, near, mine, theirs, spot, clip_index)
@@ -400,7 +436,7 @@
         name="unpack",
         out_specs=[in_hbm] * 4,
         out_shape=[jax.ShapeDtypeStruct((n, width), bf16)] * 4,
-        scratch_shapes=[vmem((n, width), bf16)] * 4 + [pltpu.SemaphoreType.DMA((4,))],
+        scratch_shapes=[vmem((n, width), bf16)] * 4 + [pltpu.SemaphoreType.DMA((4, 2))],
         compiler_params=pltpu.CompilerParams(vmem_limit_bytes=24 * MB),
     )(back, query_in, key_in, *small)
 

time: 240 us -> 239 us (level)
  no operation moved by 1% of the time
where the time goes in v4:
time: 239 us
  blocking collectives  122 us (51%)
  waiting for transfers between devices  62.2 us (26%)
  starting transfers between devices  33.4 us (14%)
  Pallas kernels  19.3 us (8%)
    all_to_all x1, blocking collectives, exchange(): lax.all_to_all(flat, ('grp', 'dp'), split_axis=0, concat_axis=0, tiled=True)  105 us
    ppermute x4, waiting for transfers between devices, z_step(): lax.ppermute(for_step(step + (half - 1) * core), ('dp', 'grp'), pairs)  56.5 us
    all_gather x1, blocking collectives, gather_codes(): here = lax.all_gather(codes, 'grp', axis=0)  17 us
    all_to_all x1, starting transfers between devices, exchange(): lax.all_to_all(flat, ('grp', 'dp'), split_axis=0, concat_axis=0, tiled=True)  16.7 us
    ppermute x4, starting transfers between devices, z_step(): lax.ppermute(for_step(step + (half - 1) * core), ('dp', 'grp'), pairs)  12.7 us
    pallas_call x1, Pallas kernels, on_device(): pl.pallas_call(attend_kernel, name='attend', in_specs=[in_hbm] + [pl.Bloc...  10.5 us
    pallas_call x1, Pallas kernels, on_device(): pl.pallas_call(functools.partial(pack_kernel, group_rows), name='pack', i...  5.66 us
  transfers between devices with their start and end apart: 9, of which 5 were waited for; matrix products, arithmetic and copies ran while one was open for 0% of the time, Pallas kernels for 0%

profile of v4, /device:TPU:1, one launch (start us, length us, event | category | flops | bytes accessed | tf_op | source)
XLA Modules:
  0.0 238.9 jit_solution(11296895913313159211)
XLA Ops:
  0.6 5.7 %pack.1 = (bf16[8,256,1024]{2,1,0:T(8,128)(2,1)}, f32[8,128]{1,0:T(8,128)}) custom-call(bf16[128,2048]{1,0:T(8,128)(2,1)} %query_ref.1, bf16[128,2048]{1,0:T(8,128)(2,1)} %key_ref.1, bf16[128,2048]{1,0:T(8,128)(2,1)} %refs_2_.1, bf16[128,2048]{1,0:T(8,128)(2,1)} %refs_3_.1, f32[1,128]{1,0:T(1,128)} %bitcast.22, f32[1,128]{1,0:T(1,128)} %bitcast.24, ...), custom_call_target="tpu_custom_call" | custom-call | tf_op jit(solution)/shard_map/pack/pallas_call | solution.py:383
  6.3 0.0 copy-start.7
  6.3 0.0 copy-start.3
  6.3 16.7 %all-to-all-start = ((bf16[256,8,1024]{2,1,0:T(8,128)(2,1)}), bf16[256,8,1024]{2,1,0:T(8,128)(2,1)}, u32[]{:S(2)}, u32[]{:S(2)}) async-start(bf16[256,8,1024]{2,1,0:T(8,128)(2,1)} %bitcast.28), calls=%async_computation | async-start | bytes 8388608 | tf_op jit(solution)/shard_map/all_to_all | solution.py:404
  23.0 0.0 copy-done.7
  23.0 17.0 %all-gather = f32[64,32]{1,0:T(8,128)S(1)} all-gather(f32[8,32]{1,0:T(8,128)S(1)} %bitcast.35), channel_id=2, replica_groups=mesh['dp'=32,'grp'=8] {'grp'}, dimensions={0}, use_global_device_ids=true | all-gather | bytes 9216 | tf_op jit(solution)/shard_map/all_gather | solution.py:333
  40.0 2.0 collective-permute-start.2
  42.0 0.0 collective-permute-start
  42.0 1.4 collective-permute-start.1
  43.5 0.1 copy.18
  43.5 0.1 stack.24
  43.7 0.2 collective-permute-done.2
  43.9 0.1 copy.21
  44.0 3.9 %collective-permute-done = f32[8,8,32]{2,1,0:T(8,128)S(1)} collective-permute-done((f32[8,8,32]{2,1,0:T(8,128)S(1)}, f32[8,8,32]{2,1,0:T(8,128)S(1)}, u32[]{:S(2)}, u32[]{:S(2)}) %collective-permute-start) | collective-permute-done | bytes 8224 | tf_op jit(solution)/shard_map/ppermute | solution.py:338
  48.0 0.1 copy.19
  48.1 0.0 collective-permute-done.1
  48.1 0.1 copy.20
  48.2 0.1 copy.23
  48.3 0.1 reshape.46
  48.5 7.6 %collective-permute-start.3 = (f32[1,8,32]{2,1,0:T(8,128)S(1)}, f32[1,8,32]{2,1,0:T(8,128)S(1)}, u32[]{:S(2)}, u32[]{:S(2)}) collective-permute-start(f32[1,8,32]{2,1,0:T(8,128)S(1)} %get-tuple-element.11), channel_id=1, source_target_pairs={{0,8},{1,33},{2,10},{3,35},{4,12},{5,37},{6,14},{7,39},{8,16},{9,4... | collective-permute-start | bytes 3080 | tf_op jit(solution)/shard_map/ppermute | solution.py:358
  56.1 0.2 collective-permute-start.6
  56.3 0.7 collective-permute-start.5
  57.0 4.2 %collective-permute-start.4 = (f32[1,8,32]{2,1,0:T(8,128)S(1)}, f32[1,8,32]{2,1,0:T(8,128)S(1)}, u32[]{:S(2)}, u32[]{:S(2)}) collective-permute-start(f32[1,8,32]{2,1,0:T(8,128)S(1)} %get-tuple-element.10), channel_id=1, source_target_pairs={{0,16},{1,41},{2,18},{3,43},{4,20},{5,45},{6,22},{7,47},{8,24},{9,... | collective-permute-start | bytes 3080 | tf_op jit(solution)/shard_map/ppermute | solution.py:358
  61.2 56.5 %collective-permute-done.3 = f32[1,8,32]{2,1,0:T(8,128)S(1)} collective-permute-done((f32[1,8,32]{2,1,0:T(8,128)S(1)}, f32[1,8,32]{2,1,0:T(8,128)S(1)}, u32[]{:S(2)}, u32[]{:S(2)}) %collective-permute-start.3) | collective-permute-done | bytes 1056 | tf_op jit(solution)/shard_map/ppermute | solution.py:358
  117.7 0.0 collective-permute-done.4
  117.7 0.0 collective-permute-done.5
  117.7 0.0 collective-permute-done.6
  117.7 0.6 collective-permute-start.7
  118.3 0.1 pad_add_fusion.spot_ref
  118.4 0.8 collective-permute-done.7.theirs_ref
  119.2 0.7 all-to-all-done
  119.9 0.0 copy-done.3
  119.9 10.5 %attend.1 = bf16[8,256,1024]{2,1,0:T(8,128)(2,1)S(1)} custom-call(bf16[8,256,1024]{2,1,0:T(8,128)(2,1)} %bitcast.4.arrived_ref, f32[1,8,32]{2,1,0:T(8,128)S(1)} %get-tuple-element.12.near_ref, f32[4,8,32]{2,1,0:T(8,128)S(1)} %constant_dynamic-update-slice_fusion.mine_ref, f32[4,8,32]{2,1,0:T(8,128)S(1)} %collective-permute-done.7.theirs_ref, ...), custom_call_target="tpu_custom_call" | custom-call | tf_op jit(solution)/shard_map/attend/pallas_call | solution.py:410
  130.4 0.0 copy-start
  130.4 0.0 copy-start.1
  130.4 0.0 copy-start.2
  130.4 0.0 copy-start.4
  130.4 0.0 copy-start.5
  130.4 0.0 copy-start.6
  130.4 105.1 %all_to_all.10 = bf16[256,8,1024]{2,1,0:T(8,128)(2,1)S(1)} all-to-all(bf16[256,8,1024]{2,1,0:T(8,128)(2,1)S(1)} %bitcast.20), channel_id=1, replica_groups=mesh['dp'=32,'grp'=8] {'grp','dp'}, dimensions={0} | all-to-all | bytes 8388608 | tf_op jit(solution)/shard_map/all_to_all | solution.py:404
  235.5 0.0 copy-done
  235.5 0.0 copy-done.1
  235.5 0.0 copy-done.2
  235.5 0.0 copy-done.4
  235.6 0.0 copy-done.5
  235.6 0.0 copy-done.6
  235.6 3.2 %unpack.1 = (bf16[128,2048]{1,0:T(8,128)(2,1)}, bf16[128,2048]{1,0:T(8,128)(2,1)}, bf16[128,2048]{1,0:T(8,128)(2,1)}, bf16[128,2048]{1,0:T(8,128)(2,1)}) custom-call(bf16[8,256,1024]{2,1,0:T(8,128)(2,1)S(1)} %bitcast.21, bf16[128,2048]{1,0:T(8,128)(2,1)S(1)} %copy-done, bf16[128,2048]{1,0:T(8,128)(2,1)S(1)} %copy-done.1, f32[1,128]{1,0:T(1,128)S(1)} %bitcast.23, ...), custom_call_target="tpu_custom_call" | custom-call | tf_op jit(solution)/shard_map/unpack/pallas_call | solution.py:434
  (6 shorter events, 0.0 us)
Async XLA Ops:
  6.3 16.7 %copy-start.7 = (f32[8,128]{1,0:T(8,128)S(1)}, f32[8,128]{1,0:T(8,128)}, u32[]{:S(2)}) copy-start(f32[8,128]{1,0:T(8,128)} %get-tuple-element.7) | copy-start | bytes 12292
  6.3 113.6 %copy-start.3 = (s32[1,1024]{1,0:T(1,128)S(1)}, s32[1,1024]{1,0:T(1,128)}, u32[]{:S(2)}) copy-start(s32[1,1024]{1,0:T(1,128)} %clip_ref.1) | copy-start | bytes 12292
  6.3 113.6 %all-to-all-start = ((bf16[256,8,1024]{2,1,0:T(8,128)(2,1)}), bf16[256,8,1024]{2,1,0:T(8,128)(2,1)}, u32[]{:S(2)}, u32[]{:S(2)}) async-start(bf16[256,8,1024]{2,1,0:T(8,128)(2,1)} %bitcast.28), calls=%async_computation | async-start | bytes 8388608 | tf_op jit(solution)/shard_map/all_to_all | solution.py:404
  40.0 3.9 %collective-permute-start.2 = (f32[8,8,32]{2,1,0:T(8,128)S(1)}, f32[8,8,32]{2,1,0:T(8,128)S(1)}, u32[]{:S(2)}, u32[]{:S(2)}) collective-permute-start(f32[8,8,32]{2,1,0:T(8,128)S(1)} %bitcast.32), channel_id=1, source_target_pairs={{0,192},{8,200},{16,208},{24,216},{32,224},{40,232},{48,240},{56,2... | collective-permute-start | bytes 24584 | tf_op jit(solution)/shard_map/ppermute | solution.py:338
  42.0 5.9 %collective-permute-start = (f32[8,8,32]{2,1,0:T(8,128)S(1)}, f32[8,8,32]{2,1,0:T(8,128)S(1)}, u32[]{:S(2)}, u32[]{:S(2)}) collective-permute-start(f32[8,8,32]{2,1,0:T(8,128)S(1)} %bitcast.33), channel_id=1, source_target_pairs={{0,64},{8,72},{16,80},{24,88},{32,96},{40,104},{48,112},{56,120},{... | collective-permute-start | bytes 24584 | tf_op jit(solution)/shard_map/ppermute | solution.py:338
  42.0 6.1 %collective-permute-start.1 = (f32[8,8,32]{2,1,0:T(8,128)S(1)}, f32[8,8,32]{2,1,0:T(8,128)S(1)}, u32[]{:S(2)}, u32[]{:S(2)}) collective-permute-start(f32[8,8,32]{2,1,0:T(8,128)S(1)} %bitcast.34), channel_id=1, source_target_pairs={{0,128},{8,136},{16,144},{24,152},{32,160},{40,168},{48,176},{56,1... | collective-permute-start | bytes 24584 | tf_op jit(solution)/shard_map/ppermute | solution.py:338
  48.5 69.2 %collective-permute-start.3 = (f32[1,8,32]{2,1,0:T(8,128)S(1)}, f32[1,8,32]{2,1,0:T(8,128)S(1)}, u32[]{:S(2)}, u32[]{:S(2)}) collective-permute-start(f32[1,8,32]{2,1,0:T(8,128)S(1)} %get-tuple-element.11), channel_id=1, source_target_pairs={{0,8},{1,33},{2,10},{3,35},{4,12},{5,37},{6,14},{7,39},{8,16},{9,4... | collective-permute-start | bytes 3080 | tf_op jit(solution)/shard_map/ppermute | solution.py:358
  56.1 61.6 %collective-permute-start.6 = (f32[1,8,32]{2,1,0:T(8,128)S(1)}, f32[1,8,32]{2,1,0:T(8,128)S(1)}, u32[]{:S(2)}, u32[]{:S(2)}) collective-permute-start(f32[1,8,32]{2,1,0:T(8,128)S(1)} %get-tuple-element.8), channel_id=1, source_target_pairs={{0,32},{1,57},{2,34},{3,59},{4,36},{5,61},{6,38},{7,63},{8,40},{9,... | collective-permute-start | bytes 3080 | tf_op jit(solution)/shard_map/ppermute | solution.py:358
  56.3 61.4 %collective-permute-start.5 = (f32[1,8,32]{2,1,0:T(8,128)S(1)}, f32[1,8,32]{2,1,0:T(8,128)S(1)}, u32[]{:S(2)}, u32[]{:S(2)}) collective-permute-start(f32[1,8,32]{2,1,0:T(8,128)S(1)} %get-tuple-element.9), channel_id=1, source_target_pairs={{0,24},{1,49},{2,26},{3,51},{4,28},{5,53},{6,30},{7,55},{8,32},{9,... | collective-permute-start | bytes 3080 | tf_op jit(solution)/shard_map/ppermute | solution.py:358
  57.0 60.7 %collective-permute-start.4 = (f32[1,8,32]{2,1,0:T(8,128)S(1)}, f32[1,8,32]{2,1,0:T(8,128)S(1)}, u32[]{:S(2)}, u32[]{:S(2)}) collective-permute-start(f32[1,8,32]{2,1,0:T(8,128)S(1)} %get-tuple-element.10), channel_id=1, source_target_pairs={{0,16},{1,41},{2,18},{3,43},{4,20},{5,45},{6,22},{7,47},{8,24},{9,... | collective-permute-start | bytes 3080 | tf_op jit(solution)/shard_map/ppermute | solution.py:358
  117.7 1.5 collective-permute-start.7
  130.4 105.2 %copy-start = (bf16[128,2048]{1,0:T(8,128)(2,1)S(1)}, bf16[128,2048]{1,0:T(8,128)(2,1)}, u32[]{:S(2)}) copy-start(bf16[128,2048]{1,0:T(8,128)(2,1)} %query_ref.1) | copy-start | bytes 1572868
  130.4 105.2 %copy-start.1 = (bf16[128,2048]{1,0:T(8,128)(2,1)S(1)}, bf16[128,2048]{1,0:T(8,128)(2,1)}, u32[]{:S(2)}) copy-start(bf16[128,2048]{1,0:T(8,128)(2,1)} %key_ref.1) | copy-start | bytes 1572868
  130.4 105.2 %copy-start.2 = (s32[3,128]{1,0:T(4,128)S(1)}, s32[3,128]{1,0:T(4,128)}, u32[]{:S(2)}) copy-start(s32[3,128]{1,0:T(4,128)} %positions_ref.1) | copy-start | bytes 4612
  130.4 105.1 %copy-start.4 = (f32[128]{0:T(128)S(1)}, f32[128]{0:T(128)}, u32[]{:S(2)}) copy-start(f32[128]{0:T(128)} %param.13) | copy-start | bytes 1540
  130.4 105.1 %copy-start.5 = (f32[128]{0:T(128)S(1)}, f32[128]{0:T(128)}, u32[]{:S(2)}) copy-start(f32[128]{0:T(128)} %param.14) | copy-start | bytes 1540
  130.4 105.1 %copy-start.6 = (s32[128]{0:T(128)S(1)}, s32[128]{0:T(128)}, u32[]{:S(2)}) copy-start(s32[128]{0:T(128)} %param.16) | copy-start | bytes 1540

commit v5 on v4

--- a/solution.py
+++ b/solution.py
@@ -136,9 +136,18 @@
             lanes = slice(start, start + HEAD_DIM)
             parts += prepared[head :: narrow // HEAD_DIM] + [value_ref[:, lanes], grad_ref[:, lanes]]
         rows = jnp.concatenate(parts, axis=1)
-        sent_ref[h] = f32_dot(pick_ref[...], rows, ((1,), (0,))).astype(jnp.bfloat16)
-        sends.append(pltpu.make_async_copy(sent_ref.at[h], out_ref.at[h], out_sems.at[h]))
-        sends[-1].start()
+        pieces = 1 if h + 1 < grp_count else 2
+        for piece in range(pieces):
+            part = pl.ds(piece * (slots // pieces), slots // pieces)
+            sent_ref[h, part, :] = f32_dot(pick_ref[part, :], rows, ((1,), (0,))).astype(
+                jnp.bfloat16
+            )
+            sends.append(
+                pltpu.make_async_copy(
+                    sent_ref.at[h, part], out_ref.at[h, part], out_sems.at[h + piece]
+                )
+            )
+            sends[-1].start()
     for send in sends:
         send.wait()
 
@@ -252,17 +261,14 @@
             grad_query.astype(bf16)
         )
         grad_key = f32_dot(query, grad_scores, ((0,), (0,))) * factor
-        by_key_ref[0, channels, :] = grad_key.astype(bf16)
-        by_key_ref[1, channels, :] = f32_dot(grad, weights_low, ((0,), (0,))).astype(bf16)
+        by_key_ref[channels, :] = grad_key.astype(bf16)
+        by_key_ref[width + head * HEAD_DIM : width + (head + 1) * HEAD_DIM, :] = f32_dot(grad, weights_low, ((0,), (0,))).astype(bf16)
 
     for g in range(grp_count):
         pick = pick_ref[g]
         part = slice(g * own, (g + 1) * own)
         out_ref[g, :, : 2 * width] = f32_dot(pick, by_query_ref[part, :], ((1,), (0,))).astype(bf16)
-        for index in range(2):
-            out_ref[g, :, (2 + index) * width : (3 + index) * width] = f32_dot(
-                pick, by_key_ref[index, :, part], ((1,), (1,))
-            ).astype(bf16)
+        out_ref[g, :, 2 * width :] = f32_dot(pick, by_key_ref[:, part], ((1,), (1,))).astype(bf16)
 
 
 def unpack_kernel(
@@ -394,7 +400,7 @@
             vmem(sent_shape, bf16),
             vmem((slots, n), bf16),
             pltpu.SemaphoreType.DMA((8,)),
-            pltpu.SemaphoreType.DMA((grp_count,)),
+            pltpu.SemaphoreType.DMA((grp_count + 1,)),
         ],
         compiler_params=pltpu.CompilerParams(vmem_limit_bytes=60 * MB),
     )(*arguments)
@@ -423,7 +429,7 @@
             vmem((group_rows, HEAD_DIM), bf16),
             vmem((group_rows, HEAD_DIM), bf16),
             vmem((group_rows, 2 * narrow), bf16),
-            vmem((2, narrow, group_rows), bf16),
+            vmem((2 * narrow, group_rows), bf16),
             pltpu.SemaphoreType.DMA((narrow // HEAD_DIM,)),
         ],
         compiler_params=pltpu.CompilerParams(vmem_limit_bytes=40 * MB),

time: 239 us -> 239 us (level)
  no operation moved by 1% of the time
where the time goes in v5:
time: 239 us
  blocking collectives  122 us (51%)
  waiting for transfers between devices  62.2 us (26%)
  starting transfers between devices  33.4 us (14%)
  Pallas kernels  19.2 us (8%)
    all_to_all x1, blocking collectives, exchange(): lax.all_to_all(flat, ('grp', 'dp'), split_axis=0, concat_axis=0, tiled=True)  105 us
    ppermute x4, waiting for transfers between devices, z_step(): lax.ppermute(for_step(step + (half - 1) * core), ('dp', 'grp'), pairs)  56.5 us
    all_gather x1, blocking collectives, gather_codes(): here = lax.all_gather(codes, 'grp', axis=0)  17 us
    all_to_all x1, starting transfers between devices, exchange(): lax.all_to_all(flat, ('grp', 'dp'), split_axis=0, concat_axis=0, tiled=True)  16.7 us
    ppermute x4, starting transfers between devices, z_step(): lax.ppermute(for_step(step + (half - 1) * core), ('dp', 'grp'), pairs)  12.7 us
    pallas_call x1, Pallas kernels, on_device(): pl.pallas_call(attend_kernel, name='attend', in_specs=[in_hbm] + [pl.Bloc...  10.5 us
    pallas_call x1, Pallas kernels, on_device(): pl.pallas_call(functools.partial(pack_kernel, group_rows), name='pack', i...  5.6 us
  transfers between devices with their start and end apart: 9, of which 5 were waited for; matrix products, arithmetic and copies ran while one was open for 0% of the time, Pallas kernels for 0%

profile of v5, /device:TPU:1, one launch (start us, length us, event | category | flops | bytes accessed | tf_op | source)
XLA Modules:
  0.0 238.9 jit_solution(15408246398993634481)
XLA Ops:
  0.6 5.6 %pack.1 = (bf16[8,256,1024]{2,1,0:T(8,128)(2,1)}, f32[8,128]{1,0:T(8,128)}) custom-call(bf16[128,2048]{1,0:T(8,128)(2,1)} %query_ref.1, bf16[128,2048]{1,0:T(8,128)(2,1)} %key_ref.1, bf16[128,2048]{1,0:T(8,128)(2,1)} %refs_2_.1, bf16[128,2048]{1,0:T(8,128)(2,1)} %refs_3_.1, f32[1,128]{1,0:T(1,128)} %bitcast.22, f32[1,128]{1,0:T(1,128)} %bitcast.24, ...), custom_call_target="tpu_custom_call" | custom-call | tf_op jit(solution)/shard_map/pack/pallas_call | solution.py:389
  6.2 0.0 copy-start.7
  6.2 0.0 copy-start.3
  6.3 16.7 %all-to-all-start = ((bf16[256,8,1024]{2,1,0:T(8,128)(2,1)}), bf16[256,8,1024]{2,1,0:T(8,128)(2,1)}, u32[]{:S(2)}, u32[]{:S(2)}) async-start(bf16[256,8,1024]{2,1,0:T(8,128)(2,1)} %bitcast.28), calls=%async_computation | async-start | bytes 8388608 | tf_op jit(solution)/shard_map/all_to_all | solution.py:410
  22.9 0.0 copy-done.7
  22.9 17.0 %all-gather = f32[64,32]{1,0:T(8,128)S(1)} all-gather(f32[8,32]{1,0:T(8,128)S(1)} %bitcast.35), channel_id=2, replica_groups=mesh['dp'=32,'grp'=8] {'grp'}, dimensions={0}, use_global_device_ids=true | all-gather | bytes 9216 | tf_op jit(solution)/shard_map/all_gather | solution.py:339
  40.0 2.0 collective-permute-start.2
  42.0 0.0 collective-permute-start
  42.0 1.4 collective-permute-start.1
  43.4 0.1 copy.18
  43.5 0.1 stack.24
  43.6 0.2 collective-permute-done.2
  43.9 0.1 copy.21
  44.0 3.9 %collective-permute-done = f32[8,8,32]{2,1,0:T(8,128)S(1)} collective-permute-done((f32[8,8,32]{2,1,0:T(8,128)S(1)}, f32[8,8,32]{2,1,0:T(8,128)S(1)}, u32[]{:S(2)}, u32[]{:S(2)}) %collective-permute-start) | collective-permute-done | bytes 8224 | tf_op jit(solution)/shard_map/ppermute | solution.py:344
  47.9 0.1 copy.19
  48.0 0.0 collective-permute-done.1
  48.0 0.1 copy.20
  48.2 0.1 copy.23
  48.3 0.1 reshape.46
  48.4 7.6 %collective-permute-start.3 = (f32[1,8,32]{2,1,0:T(8,128)S(1)}, f32[1,8,32]{2,1,0:T(8,128)S(1)}, u32[]{:S(2)}, u32[]{:S(2)}) collective-permute-start(f32[1,8,32]{2,1,0:T(8,128)S(1)} %get-tuple-element.11), channel_id=1, source_target_pairs={{0,8},{1,33},{2,10},{3,35},{4,12},{5,37},{6,14},{7,39},{8,16},{9,4... | collective-permute-start | bytes 3080 | tf_op jit(solution)/shard_map/ppermute | solution.py:364
  56.1 0.2 collective-permute-start.6
  56.2 0.7 collective-permute-start.5
  57.0 4.2 %collective-permute-start.4 = (f32[1,8,32]{2,1,0:T(8,128)S(1)}, f32[1,8,32]{2,1,0:T(8,128)S(1)}, u32[]{:S(2)}, u32[]{:S(2)}) collective-permute-start(f32[1,8,32]{2,1,0:T(8,128)S(1)} %get-tuple-element.10), channel_id=1, source_target_pairs={{0,16},{1,41},{2,18},{3,43},{4,20},{5,45},{6,22},{7,47},{8,24},{9,... | collective-permute-start | bytes 3080 | tf_op jit(solution)/shard_map/ppermute | solution.py:364
  61.1 56.5 %collective-permute-done.3 = f32[1,8,32]{2,1,0:T(8,128)S(1)} collective-permute-done((f32[1,8,32]{2,1,0:T(8,128)S(1)}, f32[1,8,32]{2,1,0:T(8,128)S(1)}, u32[]{:S(2)}, u32[]{:S(2)}) %collective-permute-start.3) | collective-permute-done | bytes 1056 | tf_op jit(solution)/shard_map/ppermute | solution.py:364
  117.6 0.0 collective-permute-done.4
  117.6 0.0 collective-permute-done.5
  117.7 0.0 collective-permute-done.6
  117.7 0.6 collective-permute-start.7
  118.3 0.1 pad_add_fusion.spot_ref
  118.4 0.8 collective-permute-done.7.theirs_ref
  119.1 0.7 all-to-all-done
  119.8 0.0 copy-done.3
  119.8 10.5 %attend.1 = bf16[8,256,1024]{2,1,0:T(8,128)(2,1)S(1)} custom-call(bf16[8,256,1024]{2,1,0:T(8,128)(2,1)} %bitcast.4.arrived_ref, f32[1,8,32]{2,1,0:T(8,128)S(1)} %get-tuple-element.12.near_ref, f32[4,8,32]{2,1,0:T(8,128)S(1)} %constant_dynamic-update-slice_fusion.mine_ref, f32[4,8,32]{2,1,0:T(8,128)S(1)} %collective-permute-done.7.theirs_ref, ...), custom_call_target="tpu_custom_call" | custom-call | tf_op jit(solution)/shard_map/attend/pallas_call | solution.py:416
  130.3 0.0 copy-start
  130.3 0.0 copy-start.1
  130.3 0.0 copy-start.2
  130.3 0.0 copy-start.4
  130.3 0.0 copy-start.5
  130.4 0.0 copy-start.6
  130.4 105.1 %all_to_all.10 = bf16[256,8,1024]{2,1,0:T(8,128)(2,1)S(1)} all-to-all(bf16[256,8,1024]{2,1,0:T(8,128)(2,1)S(1)} %bitcast.20), channel_id=1, replica_groups=mesh['dp'=32,'grp'=8] {'grp','dp'}, dimensions={0} | all-to-all | bytes 8388608 | tf_op jit(solution)/shard_map/all_to_all | solution.py:410
  235.5 0.0 copy-done
  235.5 0.0 copy-done.1
  235.5 0.0 copy-done.2
  235.5 0.0 copy-done.4
  235.5 0.0 copy-done.5
  235.5 0.0 copy-done.6
  235.5 3.2 %unpack.1 = (bf16[128,2048]{1,0:T(8,128)(2,1)}, bf16[128,2048]{1,0:T(8,128)(2,1)}, bf16[128,2048]{1,0:T(8,128)(2,1)}, bf16[128,2048]{1,0:T(8,128)(2,1)}) custom-call(bf16[8,256,1024]{2,1,0:T(8,128)(2,1)S(1)} %bitcast.21, bf16[128,2048]{1,0:T(8,128)(2,1)S(1)} %copy-done, bf16[128,2048]{1,0:T(8,128)(2,1)S(1)} %copy-done.1, f32[1,128]{1,0:T(1,128)S(1)} %bitcast.23, ...), custom_call_target="tpu_custom_call" | custom-call | tf_op jit(solution)/shard_map/unpack/pallas_call | solution.py:440
  (6 shorter events, 0.0 us)
Async XLA Ops:
  6.2 16.7 %copy-start.7 = (f32[8,128]{1,0:T(8,128)S(1)}, f32[8,128]{1,0:T(8,128)}, u32[]{:S(2)}) copy-start(f32[8,128]{1,0:T(8,128)} %get-tuple-element.7) | copy-start | bytes 12292
  6.2 113.6 %copy-start.3 = (s32[1,1024]{1,0:T(1,128)S(1)}, s32[1,1024]{1,0:T(1,128)}, u32[]{:S(2)}) copy-start(s32[1,1024]{1,0:T(1,128)} %clip_ref.1) | copy-start | bytes 12292
  6.3 113.6 %all-to-all-start = ((bf16[256,8,1024]{2,1,0:T(8,128)(2,1)}), bf16[256,8,1024]{2,1,0:T(8,128)(2,1)}, u32[]{:S(2)}, u32[]{:S(2)}) async-start(bf16[256,8,1024]{2,1,0:T(8,128)(2,1)} %bitcast.28), calls=%async_computation | async-start | bytes 8388608 | tf_op jit(solution)/shard_map/all_to_all | solution.py:410
  40.0 3.9 %collective-permute-start.2 = (f32[8,8,32]{2,1,0:T(8,128)S(1)}, f32[8,8,32]{2,1,0:T(8,128)S(1)}, u32[]{:S(2)}, u32[]{:S(2)}) collective-permute-start(f32[8,8,32]{2,1,0:T(8,128)S(1)} %bitcast.32), channel_id=1, source_target_pairs={{0,192},{8,200},{16,208},{24,216},{32,224},{40,232},{48,240},{56,2... | collective-permute-start | bytes 24584 | tf_op jit(solution)/shard_map/ppermute | solution.py:344
  42.0 5.9 %collective-permute-start = (f32[8,8,32]{2,1,0:T(8,128)S(1)}, f32[8,8,32]{2,1,0:T(8,128)S(1)}, u32[]{:S(2)}, u32[]{:S(2)}) collective-permute-start(f32[8,8,32]{2,1,0:T(8,128)S(1)} %bitcast.33), channel_id=1, source_target_pairs={{0,64},{8,72},{16,80},{24,88},{32,96},{40,104},{48,112},{56,120},{... | collective-permute-start | bytes 24584 | tf_op jit(solution)/shard_map/ppermute | solution.py:344
  42.0 6.1 %collective-permute-start.1 = (f32[8,8,32]{2,1,0:T(8,128)S(1)}, f32[8,8,32]{2,1,0:T(8,128)S(1)}, u32[]{:S(2)}, u32[]{:S(2)}) collective-permute-start(f32[8,8,32]{2,1,0:T(8,128)S(1)} %bitcast.34), channel_id=1, source_target_pairs={{0,128},{8,136},{16,144},{24,152},{32,160},{40,168},{48,176},{56,1... | collective-permute-start | bytes 24584 | tf_op jit(solution)/shard_map/ppermute | solution.py:344
  48.4 69.2 %collective-permute-start.3 = (f32[1,8,32]{2,1,0:T(8,128)S(1)}, f32[1,8,32]{2,1,0:T(8,128)S(1)}, u32[]{:S(2)}, u32[]{:S(2)}) collective-permute-start(f32[1,8,32]{2,1,0:T(8,128)S(1)} %get-tuple-element.11), channel_id=1, source_target_pairs={{0,8},{1,33},{2,10},{3,35},{4,12},{5,37},{6,14},{7,39},{8,16},{9,4... | collective-permute-start | bytes 3080 | tf_op jit(solution)/shard_map/ppermute | solution.py:364
  56.1 61.6 %collective-permute-start.6 = (f32[1,8,32]{2,1,0:T(8,128)S(1)}, f32[1,8,32]{2,1,0:T(8,128)S(1)}, u32[]{:S(2)}, u32[]{:S(2)}) collective-permute-start(f32[1,8,32]{2,1,0:T(8,128)S(1)} %get-tuple-element.8), channel_id=1, source_target_pairs={{0,32},{1,57},{2,34},{3,59},{4,36},{5,61},{6,38},{7,63},{8,40},{9,... | collective-permute-start | bytes 3080 | tf_op jit(solution)/shard_map/ppermute | solution.py:364
  56.2 61.4 %collective-permute-start.5 = (f32[1,8,32]{2,1,0:T(8,128)S(1)}, f32[1,8,32]{2,1,0:T(8,128)S(1)}, u32[]{:S(2)}, u32[]{:S(2)}) collective-permute-start(f32[1,8,32]{2,1,0:T(8,128)S(1)} %get-tuple-element.9), channel_id=1, source_target_pairs={{0,24},{1,49},{2,26},{3,51},{4,28},{5,53},{6,30},{7,55},{8,32},{9,... | collective-permute-start | bytes 3080 | tf_op jit(solution)/shard_map/ppermute | solution.py:364
  57.0 60.7 %collective-permute-start.4 = (f32[1,8,32]{2,1,0:T(8,128)S(1)}, f32[1,8,32]{2,1,0:T(8,128)S(1)}, u32[]{:S(2)}, u32[]{:S(2)}) collective-permute-start(f32[1,8,32]{2,1,0:T(8,128)S(1)} %get-tuple-element.10), channel_id=1, source_target_pairs={{0,16},{1,41},{2,18},{3,43},{4,20},{5,45},{6,22},{7,47},{8,24},{9,... | collective-permute-start | bytes 3080 | tf_op jit(solution)/shard_map/ppermute | solution.py:364
  117.7 1.5 collective-permute-start.7
  130.3 105.2 %copy-start = (bf16[128,2048]{1,0:T(8,128)(2,1)S(1)}, bf16[128,2048]{1,0:T(8,128)(2,1)}, u32[]{:S(2)}) copy-start(bf16[128,2048]{1,0:T(8,128)(2,1)} %query_ref.1) | copy-start | bytes 1572868
  130.3 105.2 %copy-start.1 = (bf16[128,2048]{1,0:T(8,128)(2,1)S(1)}, bf16[128,2048]{1,0:T(8,128)(2,1)}, u32[]{:S(2)}) copy-start(bf16[128,2048]{1,0:T(8,128)(2,1)} %key_ref.1) | copy-start | bytes 1572868
  130.3 105.2 %copy-start.2 = (s32[3,128]{1,0:T(4,128)S(1)}, s32[3,128]{1,0:T(4,128)}, u32[]{:S(2)}) copy-start(s32[3,128]{1,0:T(4,128)} %positions_ref.1) | copy-start | bytes 4612
  130.3 105.1 %copy-start.4 = (f32[128]{0:T(128)S(1)}, f32[128]{0:T(128)}, u32[]{:S(2)}) copy-start(f32[128]{0:T(128)} %param.13) | copy-start | bytes 1540
  130.3 105.1 %copy-start.5 = (f32[128]{0:T(128)S(1)}, f32[128]{0:T(128)}, u32[]{:S(2)}) copy-start(f32[128]{0:T(128)} %param.14) | copy-start | bytes 1540
  130.4 105.1 %copy-start.6 = (s32[128]{0:T(128)S(1)}, s32[128]{0:T(128)}, u32[]{:S(2)}) copy-start(s32[128]{0:T(128)} %param.16) | copy-start | bytes 1540

commit v6 on v5

--- a/solution.py
+++ b/solution.py
@@ -286,7 +286,7 @@
     grp_count, slots, _ = back_ref.shape
     n, width = query_ref.shape
     narrow = width // grp_count
-    half = grp_count // 2
+    half = grp_count // 4
 
     def send(index, h):
         lanes = pl.ds((h // half) * half * narrow, half * narrow)
@@ -328,7 +328,7 @@
             if h % half == half - 1:
                 send(index, h).start()
     for index in range(4):
-        for h in (0, half):
+        for h in range(0, grp_count, half):
             send(index, h).wait()
 
 
@@ -442,7 +442,7 @@
         name="unpack",
         out_specs=[in_hbm] * 4,
         out_shape=[jax.ShapeDtypeStruct((n, width), bf16)] * 4,
-        scratch_shapes=[vmem((n, width), bf16)] * 4 + [pltpu.SemaphoreType.DMA((4, 2))],
+        scratch_shapes=[vmem((n, width), bf16)] * 4 + [pltpu.SemaphoreType.DMA((4, 4))],
         compiler_params=pltpu.CompilerParams(vmem_limit_bytes=24 * MB),
     )(back, query_in, key_in, *small)
 

time: 239 us -> 239 us (level)
  no operation moved by 1% of the time
where the time goes in v6:
time: 239 us
  blocking collectives  122 us (51%)
  waiting for transfers between devices  62.2 us (26%)
  starting transfers between devices  33.4 us (14%)
  Pallas kernels  19.3 us (8%)
    all_to_all x1, blocking collectives, exchange(): lax.all_to_all(flat, ('grp', 'dp'), split_axis=0, concat_axis=0, tiled=True)  105 us
    ppermute x4, waiting for transfers between devices, z_step(): lax.ppermute(for_step(step + (half - 1) * core), ('dp', 'grp'), pairs)  56.5 us
    all_gather x1, blocking collectives, gather_codes(): here = lax.all_gather(codes, 'grp', axis=0)  17 us
    all_to_all x1, starting transfers between devices, exchange(): lax.all_to_all(flat, ('grp', 'dp'), split_axis=0, concat_axis=0, tiled=True)  16.7 us
    ppermute x4, starting transfers between devices, z_step(): lax.ppermute(for_step(step + (half - 1) * core), ('dp', 'grp'), pairs)  12.7 us
    pallas_call x1, Pallas kernels, on_device(): pl.pallas_call(attend_kernel, name='attend', in_specs=[in_hbm] + [pl.Bloc...  10.5 us
    pallas_call x1, Pallas kernels, on_device(): pl.pallas_call(functools.partial(pack_kernel, group_rows), name='pack', i...  5.6 us
  transfers between devices with their start and end apart: 9, of which 5 were waited for; matrix products, arithmetic and copies ran while one was open for 0% of the time, Pallas kernels for 0%

profile of v6, /device:TPU:1, one launch (start us, length us, event | category | flops | bytes accessed | tf_op | source)
XLA Modules:
  0.0 238.9 jit_solution(13776705963333616661)
XLA Ops:
  0.6 5.6 %pack.1 = (bf16[8,256,1024]{2,1,0:T(8,128)(2,1)}, f32[8,128]{1,0:T(8,128)}) custom-call(bf16[128,2048]{1,0:T(8,128)(2,1)} %query_ref.1, bf16[128,2048]{1,0:T(8,128)(2,1)} %key_ref.1, bf16[128,2048]{1,0:T(8,128)(2,1)} %refs_2_.1, bf16[128,2048]{1,0:T(8,128)(2,1)} %refs_3_.1, f32[1,128]{1,0:T(1,128)} %bitcast.22, f32[1,128]{1,0:T(1,128)} %bitcast.24, ...), custom_call_target="tpu_custom_call" | custom-call | tf_op jit(solution)/shard_map/pack/pallas_call | solution.py:389
  6.2 0.0 copy-start.7
  6.2 0.0 copy-start.3
  6.3 16.7 %all-to-all-start = ((bf16[256,8,1024]{2,1,0:T(8,128)(2,1)}), bf16[256,8,1024]{2,1,0:T(8,128)(2,1)}, u32[]{:S(2)}, u32[]{:S(2)}) async-start(bf16[256,8,1024]{2,1,0:T(8,128)(2,1)} %bitcast.28), calls=%async_computation | async-start | bytes 8388608 | tf_op jit(solution)/shard_map/all_to_all | solution.py:410
  22.9 0.0 copy-done.7
  22.9 17.0 %all-gather = f32[64,32]{1,0:T(8,128)S(1)} all-gather(f32[8,32]{1,0:T(8,128)S(1)} %bitcast.35), channel_id=2, replica_groups=mesh['dp'=32,'grp'=8] {'grp'}, dimensions={0}, use_global_device_ids=true | all-gather | bytes 9216 | tf_op jit(solution)/shard_map/all_gather | solution.py:339
  40.0 2.0 collective-permute-start.2
  42.0 0.0 collective-permute-start
  42.0 1.4 collective-permute-start.1
  43.4 0.1 copy.18
  43.5 0.1 stack.24
  43.6 0.2 collective-permute-done.2
  43.9 0.1 copy.21
  44.0 3.9 %collective-permute-done = f32[8,8,32]{2,1,0:T(8,128)S(1)} collective-permute-done((f32[8,8,32]{2,1,0:T(8,128)S(1)}, f32[8,8,32]{2,1,0:T(8,128)S(1)}, u32[]{:S(2)}, u32[]{:S(2)}) %collective-permute-start) | collective-permute-done | bytes 8224 | tf_op jit(solution)/shard_map/ppermute | solution.py:344
  47.9 0.1 copy.19
  48.0 0.0 collective-permute-done.1
  48.0 0.1 copy.20
  48.2 0.1 copy.23
  48.3 0.1 reshape.46
  48.4 7.6 %collective-permute-start.3 = (f32[1,8,32]{2,1,0:T(8,128)S(1)}, f32[1,8,32]{2,1,0:T(8,128)S(1)}, u32[]{:S(2)}, u32[]{:S(2)}) collective-permute-start(f32[1,8,32]{2,1,0:T(8,128)S(1)} %get-tuple-element.11), channel_id=1, source_target_pairs={{0,8},{1,33},{2,10},{3,35},{4,12},{5,37},{6,14},{7,39},{8,16},{9,4... | collective-permute-start | bytes 3080 | tf_op jit(solution)/shard_map/ppermute | solution.py:364
  56.1 0.2 collective-permute-start.6
  56.2 0.7 collective-permute-start.5
  57.0 4.2 %collective-permute-start.4 = (f32[1,8,32]{2,1,0:T(8,128)S(1)}, f32[1,8,32]{2,1,0:T(8,128)S(1)}, u32[]{:S(2)}, u32[]{:S(2)}) collective-permute-start(f32[1,8,32]{2,1,0:T(8,128)S(1)} %get-tuple-element.10), channel_id=1, source_target_pairs={{0,16},{1,41},{2,18},{3,43},{4,20},{5,45},{6,22},{7,47},{8,24},{9,... | collective-permute-start | bytes 3080 | tf_op jit(solution)/shard_map/ppermute | solution.py:364
  61.1 56.5 %collective-permute-done.3 = f32[1,8,32]{2,1,0:T(8,128)S(1)} collective-permute-done((f32[1,8,32]{2,1,0:T(8,128)S(1)}, f32[1,8,32]{2,1,0:T(8,128)S(1)}, u32[]{:S(2)}, u32[]{:S(2)}) %collective-permute-start.3) | collective-permute-done | bytes 1056 | tf_op jit(solution)/shard_map/ppermute | solution.py:364
  117.6 0.0 collective-permute-done.4
  117.6 0.0 collective-permute-done.5
  117.7 0.0 collective-permute-done.6
  117.7 0.6 collective-permute-start.7
  118.3 0.1 pad_add_fusion.spot_ref
  118.4 0.8 collective-permute-done.7.theirs_ref
  119.1 0.7 all-to-all-done
  119.8 0.0 copy-done.3
  119.8 10.5 %attend.1 = bf16[8,256,1024]{2,1,0:T(8,128)(2,1)S(1)} custom-call(bf16[8,256,1024]{2,1,0:T(8,128)(2,1)} %bitcast.4.arrived_ref, f32[1,8,32]{2,1,0:T(8,128)S(1)} %get-tuple-element.12.near_ref, f32[4,8,32]{2,1,0:T(8,128)S(1)} %constant_dynamic-update-slice_fusion.mine_ref, f32[4,8,32]{2,1,0:T(8,128)S(1)} %collective-permute-done.7.theirs_ref, ...), custom_call_target="tpu_custom_call" | custom-call | tf_op jit(solution)/shard_map/attend/pallas_call | solution.py:416
  130.3 0.0 copy-start
  130.3 0.0 copy-start.1
  130.3 0.0 copy-start.2
  130.3 0.0 copy-start.4
  130.3 0.0 copy-start.5
  130.4 0.0 copy-start.6
  130.4 105.1 %all_to_all.10 = bf16[256,8,1024]{2,1,0:T(8,128)(2,1)S(1)} all-to-all(bf16[256,8,1024]{2,1,0:T(8,128)(2,1)S(1)} %bitcast.20), channel_id=1, replica_groups=mesh['dp'=32,'grp'=8] {'grp','dp'}, dimensions={0} | all-to-all | bytes 8388608 | tf_op jit(solution)/shard_map/all_to_all | solution.py:410
  235.5 0.0 copy-done
  235.5 0.0 copy-done.1
  235.5 0.0 copy-done.2
  235.5 0.0 copy-done.4
  235.5 0.0 copy-done.5
  235.5 0.0 copy-done.6
  235.5 3.2 %unpack.1 = (bf16[128,2048]{1,0:T(8,128)(2,1)}, bf16[128,2048]{1,0:T(8,128)(2,1)}, bf16[128,2048]{1,0:T(8,128)(2,1)}, bf16[128,2048]{1,0:T(8,128)(2,1)}) custom-call(bf16[8,256,1024]{2,1,0:T(8,128)(2,1)S(1)} %bitcast.21, bf16[128,2048]{1,0:T(8,128)(2,1)S(1)} %copy-done, bf16[128,2048]{1,0:T(8,128)(2,1)S(1)} %copy-done.1, f32[1,128]{1,0:T(1,128)S(1)} %bitcast.23, ...), custom_call_target="tpu_custom_call" | custom-call | tf_op jit(solution)/shard_map/unpack/pallas_call | solution.py:440
  (6 shorter events, 0.0 us)
Async XLA Ops:
  6.2 16.7 %copy-start.7 = (f32[8,128]{1,0:T(8,128)S(1)}, f32[8,128]{1,0:T(8,128)}, u32[]{:S(2)}) copy-start(f32[8,128]{1,0:T(8,128)} %get-tuple-element.7) | copy-start | bytes 12292
  6.2 113.6 %copy-start.3 = (s32[1,1024]{1,0:T(1,128)S(1)}, s32[1,1024]{1,0:T(1,128)}, u32[]{:S(2)}) copy-start(s32[1,1024]{1,0:T(1,128)} %clip_ref.1) | copy-start | bytes 12292
  6.3 113.6 %all-to-all-start = ((bf16[256,8,1024]{2,1,0:T(8,128)(2,1)}), bf16[256,8,1024]{2,1,0:T(8,128)(2,1)}, u32[]{:S(2)}, u32[]{:S(2)}) async-start(bf16[256,8,1024]{2,1,0:T(8,128)(2,1)} %bitcast.28), calls=%async_computation | async-start | bytes 8388608 | tf_op jit(solution)/shard_map/all_to_all | solution.py:410
  40.0 3.9 %collective-permute-start.2 = (f32[8,8,32]{2,1,0:T(8,128)S(1)}, f32[8,8,32]{2,1,0:T(8,128)S(1)}, u32[]{:S(2)}, u32[]{:S(2)}) collective-permute-start(f32[8,8,32]{2,1,0:T(8,128)S(1)} %bitcast.32), channel_id=1, source_target_pairs={{0,192},{8,200},{16,208},{24,216},{32,224},{40,232},{48,240},{56,2... | collective-permute-start | bytes 24584 | tf_op jit(solution)/shard_map/ppermute | solution.py:344
  42.0 5.9 %collective-permute-start = (f32[8,8,32]{2,1,0:T(8,128)S(1)}, f32[8,8,32]{2,1,0:T(8,128)S(1)}, u32[]{:S(2)}, u32[]{:S(2)}) collective-permute-start(f32[8,8,32]{2,1,0:T(8,128)S(1)} %bitcast.33), channel_id=1, source_target_pairs={{0,64},{8,72},{16,80},{24,88},{32,96},{40,104},{48,112},{56,120},{... | collective-permute-start | bytes 24584 | tf_op jit(solution)/shard_map/ppermute | solution.py:344
  42.0 6.1 %collective-permute-start.1 = (f32[8,8,32]{2,1,0:T(8,128)S(1)}, f32[8,8,32]{2,1,0:T(8,128)S(1)}, u32[]{:S(2)}, u32[]{:S(2)}) collective-permute-start(f32[8,8,32]{2,1,0:T(8,128)S(1)} %bitcast.34), channel_id=1, source_target_pairs={{0,128},{8,136},{16,144},{24,152},{32,160},{40,168},{48,176},{56,1... | collective-permute-start | bytes 24584 | tf_op jit(solution)/shard_map/ppermute | solution.py:344
  48.4 69.2 %collective-permute-start.3 = (f32[1,8,32]{2,1,0:T(8,128)S(1)}, f32[1,8,32]{2,1,0:T(8,128)S(1)}, u32[]{:S(2)}, u32[]{:S(2)}) collective-permute-start(f32[1,8,32]{2,1,0:T(8,128)S(1)} %get-tuple-element.11), channel_id=1, source_target_pairs={{0,8},{1,33},{2,10},{3,35},{4,12},{5,37},{6,14},{7,39},{8,16},{9,4... | collective-permute-start | bytes 3080 | tf_op jit(solution)/shard_map/ppermute | solution.py:364
  56.1 61.6 %collective-permute-start.6 = (f32[1,8,32]{2,1,0:T(8,128)S(1)}, f32[1,8,32]{2,1,0:T(8,128)S(1)}, u32[]{:S(2)}, u32[]{:S(2)}) collective-permute-start(f32[1,8,32]{2,1,0:T(8,128)S(1)} %get-tuple-element.8), channel_id=1, source_target_pairs={{0,32},{1,57},{2,34},{3,59},{4,36},{5,61},{6,38},{7,63},{8,40},{9,... | collective-permute-start | bytes 3080 | tf_op jit(solution)/shard_map/ppermute | solution.py:364
  56.2 61.4 %collective-permute-start.5 = (f32[1,8,32]{2,1,0:T(8,128)S(1)}, f32[1,8,32]{2,1,0:T(8,128)S(1)}, u32[]{:S(2)}, u32[]{:S(2)}) collective-permute-start(f32[1,8,32]{2,1,0:T(8,128)S(1)} %get-tuple-element.9), channel_id=1, source_target_pairs={{0,24},{1,49},{2,26},{3,51},{4,28},{5,53},{6,30},{7,55},{8,32},{9,... | collective-permute-start | bytes 3080 | tf_op jit(solution)/shard_map/ppermute | solution.py:364
  57.0 60.7 %collective-permute-start.4 = (f32[1,8,32]{2,1,0:T(8,128)S(1)}, f32[1,8,32]{2,1,0:T(8,128)S(1)}, u32[]{:S(2)}, u32[]{:S(2)}) collective-permute-start(f32[1,8,32]{2,1,0:T(8,128)S(1)} %get-tuple-element.10), channel_id=1, source_target_pairs={{0,16},{1,41},{2,18},{3,43},{4,20},{5,45},{6,22},{7,47},{8,24},{9,... | collective-permute-start | bytes 3080 | tf_op jit(solution)/shard_map/ppermute | solution.py:364
  117.7 1.5 collective-permute-start.7
  130.3 105.2 %copy-start = (bf16[128,2048]{1,0:T(8,128)(2,1)S(1)}, bf16[128,2048]{1,0:T(8,128)(2,1)}, u32[]{:S(2)}) copy-start(bf16[128,2048]{1,0:T(8,128)(2,1)} %query_ref.1) | copy-start | bytes 1572868
  130.3 105.2 %copy-start.1 = (bf16[128,2048]{1,0:T(8,128)(2,1)S(1)}, bf16[128,2048]{1,0:T(8,128)(2,1)}, u32[]{:S(2)}) copy-start(bf16[128,2048]{1,0:T(8,128)(2,1)} %key_ref.1) | copy-start | bytes 1572868
  130.3 105.2 %copy-start.2 = (s32[3,128]{1,0:T(4,128)S(1)}, s32[3,128]{1,0:T(4,128)}, u32[]{:S(2)}) copy-start(s32[3,128]{1,0:T(4,128)} %positions_ref.1) | copy-start | bytes 4612
  130.3 105.1 %copy-start.4 = (f32[128]{0:T(128)S(1)}, f32[128]{0:T(128)}, u32[]{:S(2)}) copy-start(f32[128]{0:T(128)} %param.13) | copy-start | bytes 1540
  130.3 105.1 %copy-start.5 = (f32[128]{0:T(128)S(1)}, f32[128]{0:T(128)}, u32[]{:S(2)}) copy-start(f32[128]{0:T(128)} %param.14) | copy-start | bytes 1540
  130.4 105.1 %copy-start.6 = (s32[128]{0:T(128)S(1)}, s32[128]{0:T(128)}, u32[]{:S(2)}) copy-start(s32[128]{0:T(128)} %param.16) | copy-start | bytes 1540
